TPU v7x, 32 devices: a whole 2x2x4 slice. The times are simulated.
32 devices in a mesh: dp: 8 (over z, x), row: 2 (over y), col: 2 (over core).
Axes of the slice: x: 2, y: 2, z: 4, core: 2. Of those that a mesh axis runs over, the one named last changes fastest.
Arguments:
- tokens: bfloat16 [25216, 768], P(('dp', 'row', 'col')), may hold values from -6 to 6
- out_grad: bfloat16 [25216, 768], P(('dp', 'row', 'col')), may hold values from -6 to 6
- routes: int32 [25216, 2], P(('dp', 'row', 'col')), may hold values from 0 to 15, all different within a row
- slot_order: int32 [32, 1576], P(('dp', 'row', 'col')), may hold values from 0 to 1575, each once within a row
- norm_params: float32 [768, 4], P(('dp', 'row', 'col')), may hold values from -0.5 to 5
- qkv_weight: float32 [768, 3, 768], P(('dp', 'row', 'col')), may hold values from -0.21875 to 0.21875
- proj_weight: float32 [768, 768], P(('dp', 'row', 'col')), may hold values from -0.875 to 0.875
- router_weight: float32 [768, 16], P(('dp', 'row', 'col')), may hold values from -0.15625 to 0.15625
- inner_weight: float32 [16, 768, 3072], P(('dp', 'col'), None, 'row'), may hold values from -1 to 1
- outer_weight: float32 [16, 3072, 768], P(('dp', 'col'), 'row'), may hold values from -0.15625 to 0.15625
- norm_moment: float32 [768, 4], P(('dp', 'row', 'col')), may hold values from -1 to 1
- norm_second: float32 [768, 4], P(('dp', 'row', 'col')), may hold values from 0 to 1, as said below
- qkv_moment: float32 [768, 3, 768], P(('dp', 'row', 'col')), may hold values from -1 to 1
- qkv_second: float32 [768, 3, 768], P(('dp', 'row', 'col')), may hold values from 0 to 1, as said below
- proj_moment: float32 [768, 768], P(('dp', 'row', 'col')), may hold values from -1 to 1
- proj_second: float32 [768, 768], P(('dp', 'row', 'col')), may hold values from 0 to 1, as said below
- router_moment: float32 [768, 16], P(('dp', 'row', 'col')), may hold values from -1 to 1
- router_second: float32 [768, 16], P(('dp', 'row', 'col')), may hold values from 0 to 1, as said below
- inner_moment: float32 [16, 768, 3072], P(('dp', 'col'), None, 'row'), may hold values from -1 to 1
- inner_second: float32 [16, 768, 3072], P(('dp', 'col'), None, 'row'), may hold values from 0 to 1, as said below
- outer_moment: float32 [16, 3072, 768], P(('dp', 'col'), 'row'), may hold values from -1 to 1
- outer_second: float32 [16, 3072, 768], P(('dp', 'col'), 'row'), may hold values from 0 to 1, as said below
Outputs:
- block_out: bfloat16 [25216, 768], P(('dp', 'row', 'col'))
- tokens_grad: float32 [25216, 768], P(('dp', 'row', 'col'))
- grad_norm: float32 [], replicated
- norm_moment_new: float32 [768, 4], P(('dp', 'row', 'col'))
- norm_second_new: float32 [768, 4], P(('dp', 'row', 'col'))
- norm_params_new: float32 [768, 4], P(('dp', 'row', 'col'))
- qkv_moment_new: float32 [768, 3, 768], P(('dp', 'row', 'col'))
- qkv_second_new: float32 [768, 3, 768], P(('dp', 'row', 'col'))
- qkv_weight_new: float32 [768, 3, 768], P(('dp', 'row', 'col'))
- proj_moment_new: float32 [768, 768], P(('dp', 'row', 'col'))
- proj_second_new: float32 [768, 768], P(('dp', 'row', 'col'))
- proj_weight_new: float32 [768, 768], P(('dp', 'row', 'col'))
- router_moment_new: float32 [768, 16], P(('dp', 'row', 'col'))
- router_second_new: float32 [768, 16], P(('dp', 'row', 'col'))
- router_weight_new: float32 [768, 16], P(('dp', 'row', 'col'))
- inner_moment_new: float32 [16, 768, 3072], P(('dp', 'col'), None, 'row')
- inner_second_new: float32 [16, 768, 3072], P(('dp', 'col'), None, 'row')
- inner_weight_new: float32 [16, 768, 3072], P(('dp', 'col'), None, 'row')
- outer_moment_new: float32 [16, 3072, 768], P(('dp', 'col'), 'row')
- outer_second_new: float32 [16, 3072, 768], P(('dp', 'col'), 'row')
- outer_weight_new: float32 [16, 3072, 768], P(('dp', 'col'), 'row')
Inputs may be any that keep to these rules, and one draw needn't show every extreme that they name: `routes`: each row names 2 different experts. `slot_order`: each row is an ordering of the 1576 pairs of one device. `norm_second`: positive. `qkv_second`: positive. `proj_second`: positive. `router_second`: positive. `inner_second`: positive. `outer_second`: positive.
All inputs are finite; a program needn't handle non-finite values.
Results may differ from a plain program's by a relative error of at most 0.015.
The roundings to bfloat16 on the way count: a program that leaves them out, or rounds other values in their place, can miss the bound.
Values may be sent and summed in bfloat16 or wider, within the bound.
No kernel may reach another device: no remote copies, remote signals or barrier semaphores. Data moves between devices by JAX's collectives and lax.ppermute only.
A program may use at most 256 MiB of HBM per device.

v0:
```python
import jax
import jax.numpy as jnp
from jax import lax
from jax.sharding import PartitionSpec as P

HEADS = 12
HEAD = 64
SEQ = 197
STEP = 10


NORM_EPS = 1e-06
CLIP_NORM = 1.0
BETA_ONE = 0.9
BETA_TWO = 0.999
ADAM_EPS = 1e-08
RATE_MATRIX = 0.08
RATE_NORM = 0.4
DECAY_MATRIX = 0.1


def layer_norm(tok_rows, gain_vec, bias_vec):
    mean_val = jnp.mean(tok_rows, axis=-1, keepdims=True)
    centred = tok_rows - mean_val
    spread_val = jnp.mean(centred * centred, axis=-1, keepdims=True)
    return centred * lax.rsqrt(spread_val + NORM_EPS) * gain_vec + bias_vec


def gelu_exact(values):
    return jax.nn.gelu(values, approximate=False)


def device_slots(route_rows, order_row, expert_count, capacity):
    pair_expert = route_rows.reshape(-1)
    pair_count = pair_expert.shape[0]
    ranked = pair_expert[order_row]
    hit_table = (ranked[:, None] == jnp.arange(expert_count, dtype=jnp.int32)[None, :]).astype(
        jnp.int32
    )
    before = jnp.cumsum(hit_table, axis=0) - hit_table
    ranked_pos = jnp.sum(before * hit_table, axis=1)
    position = jnp.zeros((pair_count,), jnp.int32).at[order_row].set(ranked_pos)
    return jnp.where(
        position < capacity, pair_expert * capacity + position, expert_count * capacity
    )


def adam_update(weight, gradient, moment_one, moment_two, clip_scale, rate_val, decay_val):
    clipped = gradient * clip_scale
    first_new = BETA_ONE * moment_one + (1.0 - BETA_ONE) * clipped
    second_new = BETA_TWO * moment_two + (1.0 - BETA_TWO) * clipped * clipped
    first_hat = first_new / (1.0 - BETA_ONE**STEP)
    second_hat = second_new / (1.0 - BETA_TWO**STEP)
    return (
        first_new,
        second_new,
        weight - rate_val * (first_hat / (jnp.sqrt(second_hat) + ADAM_EPS) + decay_val * weight),
    )


def on_device(
    tokens,
    out_grad,
    routes,
    slot_order,
    norm_params,
    qkv_weight,
    proj_weight,
    router_weight,
    inner_weight,
    outer_weight,
    norm_moment,
    norm_second,
    qkv_moment,
    qkv_second,
    proj_moment,
    proj_second,
    router_moment,
    router_second,
    inner_moment,
    inner_second,
    outer_moment,
    outer_second,
):
    tok_count = tokens.shape[0]
    width = tokens.shape[1]
    choose_count = routes.shape[1]
    pair_count = tok_count * choose_count
    expert_count = router_weight.shape[1]
    local_experts = inner_weight.shape[0]
    group_count = lax.axis_size("dp") * lax.axis_size("col")
    capacity = max(2, (5 * pair_count + 4 * expert_count - 1) // (4 * expert_count))
    images = tok_count // SEQ
    head_scale = HEAD ** (-0.5)
    low_type = jnp.bfloat16
    full_type = jnp.float32
    norm_full, qkv_full, proj_full, router_full = (
        lax.all_gather(norm_params.astype(low_type), ("dp", "row", "col"), axis=0, tiled=True),
        lax.all_gather(qkv_weight.astype(low_type), ("dp", "row", "col"), axis=0, tiled=True),
        lax.all_gather(proj_weight.astype(low_type), ("dp", "row", "col"), axis=0, tiled=True),
        lax.all_gather(router_weight.astype(low_type), ("dp", "row", "col"), axis=0, tiled=True),
    )
    norm_vals = norm_full.astype(full_type)
    rows_in = tokens.astype(full_type)
    normed_one_f, back_one = jax.vjp(layer_norm, rows_in, norm_vals[:, 0], norm_vals[:, 1])
    normed_one = normed_one_f.astype(low_type)
    projected = jnp.einsum(
        "td,dsf->tsf", normed_one, qkv_full, preferred_element_type=full_type
    ).astype(low_type)
    projected = projected.reshape(images, SEQ, 3, HEADS, HEAD)
    queries = projected[:, :, 0]
    key_rows = projected[:, :, 1]
    value_rows = projected[:, :, 2]
    scores = (
        jnp.einsum("ishd,ijhd->ihsj", queries, key_rows, preferred_element_type=full_type)
        * head_scale
    )
    probs = jax.nn.softmax(scores, axis=-1)
    probs_low = probs.astype(low_type)
    mixed = jnp.einsum(
        "ihsj,ijhd->ishd", probs_low, value_rows, preferred_element_type=full_type
    ).astype(low_type)
    mixed = mixed.reshape(tok_count, width)
    after_attn = rows_in + jnp.einsum(
        "tf,of->to", mixed, proj_full, preferred_element_type=full_type
    )
    normed_two_f, back_two = jax.vjp(layer_norm, after_attn, norm_vals[:, 2], norm_vals[:, 3])
    normed_two = normed_two_f.astype(low_type)
    logits = jnp.dot(normed_two, router_full, preferred_element_type=full_type)
    gate_vals = jax.nn.softmax(jnp.take_along_axis(logits, routes, axis=1), axis=-1)
    pair_slot = device_slots(routes, slot_order[0], expert_count, capacity)
    pair_ids = jnp.arange(pair_count, dtype=jnp.int32)
    slot_pair = (
        jnp.full((expert_count * capacity + 1,), pair_count, jnp.int32)
        .at[pair_slot]
        .set(pair_ids)[:-1]
    )
    slot_token = slot_pair // choose_count
    normed_pad = jnp.concatenate([normed_two, jnp.zeros((1, width), low_type)])
    send_rows = normed_pad[slot_token].reshape(group_count, local_experts, capacity, width)
    arrived = lax.all_to_all(send_rows, ("dp", "col"), split_axis=0, concat_axis=0, tiled=True)
    inner_low = inner_weight.astype(low_type)
    outer_low = outer_weight.astype(low_type)
    inner_full, outer_full = (
        lax.all_gather(inner_low, "row", axis=2, tiled=True),
        lax.all_gather(outer_low, "row", axis=1, tiled=True),
    )
    inner_act = jnp.einsum("sjcd,jdf->sjcf", arrived, inner_full, preferred_element_type=full_type)
    hidden_f, gelu_back = jax.vjp(gelu_exact, inner_act)
    hidden = hidden_f.astype(low_type)
    expert_res = jnp.einsum("sjcf,jfd->sjcd", hidden, outer_full, preferred_element_type=full_type)
    returned = lax.all_to_all(
        expert_res.astype(low_type), ("dp", "col"), split_axis=0, concat_axis=0, tiled=True
    )
    returned_pad = jnp.concatenate(
        [returned.reshape(expert_count * capacity, width), jnp.zeros((1, width), low_type)]
    )
    pair_rows = returned_pad[pair_slot].astype(full_type).reshape(tok_count, choose_count, width)
    moe_out = jnp.sum(gate_vals[:, :, None] * pair_rows, axis=1)
    block_out = (after_attn + moe_out).astype(low_type)
    grad_out = out_grad.astype(full_type)
    grad_gate = jnp.sum(grad_out[:, None, :] * pair_rows, axis=2)
    pair_grad = (
        (gate_vals[:, :, None] * grad_out[:, None, :]).astype(low_type).reshape(pair_count, width)
    )
    pair_grad_pad = jnp.concatenate([pair_grad, jnp.zeros((1, width), low_type)])
    send_grad = pair_grad_pad[slot_pair].reshape(group_count, local_experts, capacity, width)
    grad_arrived = lax.all_to_all(send_grad, ("dp", "col"), split_axis=0, concat_axis=0, tiled=True)
    grad_hidden = jnp.einsum(
        "sjcd,jfd->sjcf", grad_arrived, outer_full, preferred_element_type=full_type
    )
    grad_inner = gelu_back(grad_hidden)[0].astype(low_type)
    inner_whole = jnp.einsum(
        "sjcd,sjcf->jdf", arrived, grad_inner, preferred_element_type=full_type
    )
    outer_whole = jnp.einsum(
        "sjcf,sjcd->jfd", hidden, grad_arrived, preferred_element_type=full_type
    )
    inner_grad, outer_grad = (
        lax.psum_scatter(
            inner_whole.astype(jnp.bfloat16), "row", scatter_dimension=2, tiled=True
        ).astype(jnp.float32),
        lax.psum_scatter(
            outer_whole.astype(jnp.bfloat16), "row", scatter_dimension=1, tiled=True
        ).astype(jnp.float32),
    )
    grad_in = jnp.einsum("sjcf,jdf->sjcd", grad_inner, inner_full, preferred_element_type=full_type)
    grad_back = lax.all_to_all(
        grad_in.astype(low_type), ("dp", "col"), split_axis=0, concat_axis=0, tiled=True
    )
    back_pad = jnp.concatenate(
        [grad_back.reshape(expert_count * capacity, width), jnp.zeros((1, width), low_type)]
    )
    pair_back = back_pad[pair_slot].astype(full_type).reshape(tok_count, choose_count, width)
    grad_chosen = gate_vals * (grad_gate - jnp.sum(gate_vals * grad_gate, axis=1, keepdims=True))
    hot_table = routes[:, :, None] == jnp.arange(expert_count, dtype=jnp.int32)[None, None, :]
    grad_logits = jnp.sum(jnp.where(hot_table, grad_chosen[:, :, None], 0.0), axis=1).astype(
        low_type
    )
    router_grad = jnp.dot(normed_two.T, grad_logits, preferred_element_type=full_type)
    grad_norm_two = jnp.dot(grad_logits, router_full.T, preferred_element_type=full_type) + jnp.sum(
        pair_back, axis=1
    )
    grad_after_ln, gain_two_grad, bias_two_grad = back_two(grad_norm_two)
    grad_after = grad_out + grad_after_ln
    grad_branch = grad_after.astype(low_type)
    proj_grad = jnp.dot(grad_branch.T, mixed, preferred_element_type=full_type)
    grad_mixed = jnp.dot(grad_branch, proj_full, preferred_element_type=full_type).astype(low_type)
    grad_mixed = grad_mixed.reshape(images, SEQ, HEADS, HEAD)
    grad_probs = jnp.einsum(
        "ishd,ijhd->ihsj", grad_mixed, value_rows, preferred_element_type=full_type
    )
    grad_values = jnp.einsum(
        "ihsj,ishd->ijhd", probs_low, grad_mixed, preferred_element_type=full_type
    )
    grad_scores = (
        probs * (grad_probs - jnp.sum(grad_probs * probs, axis=-1, keepdims=True))
    ).astype(low_type)
    grad_queries = (
        jnp.einsum("ihsj,ijhd->ishd", grad_scores, key_rows, preferred_element_type=full_type)
        * head_scale
    )
    grad_keys = (
        jnp.einsum("ihsj,ishd->ijhd", grad_scores, queries, preferred_element_type=full_type)
        * head_scale
    )
    grad_qkv = (
        jnp.stack([grad_queries, grad_keys, grad_values], axis=2)
        .astype(low_type)
        .reshape(tok_count, 3, width)
    )
    qkv_grad = jnp.einsum("td,tsf->dsf", normed_one, grad_qkv, preferred_element_type=full_type)
    grad_norm_one = jnp.einsum("tsf,dsf->td", grad_qkv, qkv_full, preferred_element_type=full_type)
    grad_rows_one, gain_one_grad, bias_one_grad = back_one(grad_norm_one)
    tokens_grad = grad_after + grad_rows_one
    norm_grad = jnp.stack([gain_one_grad, bias_one_grad, gain_two_grad, bias_two_grad], axis=1)
    norm_share, qkv_share, proj_share, router_share = (
        lax.psum_scatter(norm_grad, ("dp", "row", "col"), scatter_dimension=0, tiled=True),
        lax.psum_scatter(qkv_grad, ("dp", "row", "col"), scatter_dimension=0, tiled=True),
        lax.psum_scatter(proj_grad, ("dp", "row", "col"), scatter_dimension=0, tiled=True),
        lax.psum_scatter(router_grad, ("dp", "row", "col"), scatter_dimension=0, tiled=True),
    )
    local_square = (
        jnp.sum(norm_share * norm_share)
        + jnp.sum(qkv_share * qkv_share)
        + jnp.sum(proj_share * proj_share)
        + jnp.sum(router_share * router_share)
        + jnp.sum(inner_grad * inner_grad)
        + jnp.sum(outer_grad * outer_grad)
    )
    square_sum = lax.psum(local_square, ("dp", "row", "col"))
    grad_norm = jnp.sqrt(square_sum)
    clip_scale = jnp.minimum(1.0, CLIP_NORM / (grad_norm + 1e-06))
    norm_m, norm_s, norm_w = adam_update(
        norm_params, norm_share, norm_moment, norm_second, clip_scale, RATE_NORM, 0.0
    )
    qkv_m, qkv_s, qkv_w = adam_update(
        qkv_weight, qkv_share, qkv_moment, qkv_second, clip_scale, RATE_MATRIX, DECAY_MATRIX
    )
    proj_m, proj_s, proj_w = adam_update(
        proj_weight, proj_share, proj_moment, proj_second, clip_scale, RATE_MATRIX, DECAY_MATRIX
    )
    router_m, router_s, router_w = adam_update(
        router_weight,
        router_share,
        router_moment,
        router_second,
        clip_scale,
        RATE_MATRIX,
        DECAY_MATRIX,
    )
    inner_m, inner_s, inner_w = adam_update(
        inner_weight, inner_grad, inner_moment, inner_second, clip_scale, RATE_MATRIX, DECAY_MATRIX
    )
    outer_m, outer_s, outer_w = adam_update(
        outer_weight, outer_grad, outer_moment, outer_second, clip_scale, RATE_MATRIX, DECAY_MATRIX
    )
    return (
        block_out,
        tokens_grad,
        grad_norm,
        norm_m,
        norm_s,
        norm_w,
        qkv_m,
        qkv_s,
        qkv_w,
        proj_m,
        proj_s,
        proj_w,
        router_m,
        router_s,
        router_w,
        inner_m,
        inner_s,
        inner_w,
        outer_m,
        outer_s,
        outer_w,
    )


def solution(mesh):
    return jax.shard_map(
        on_device,
        mesh=mesh,
        in_specs=(
            P(("dp", "row", "col"), None),
            P(("dp", "row", "col"), None),
            P(("dp", "row", "col"), None),
            P(("dp", "row", "col"), None),
            P(("dp", "row", "col"), None),
            P(("dp", "row", "col"), None, None),
            P(("dp", "row", "col"), None),
            P(("dp", "row", "col"), None),
            P(("dp", "col"), None, "row"),
            P(("dp", "col"), "row", None),
            P(("dp", "row", "col"), None),
            P(("dp", "row", "col"), None),
            P(("dp", "row", "col"), None, None),
            P(("dp", "row", "col"), None, None),
            P(("dp", "row", "col"), None),
            P(("dp", "row", "col"), None),
            P(("dp", "row", "col"), None),
            P(("dp", "row", "col"), None),
            P(("dp", "col"), None, "row"),
            P(("dp", "col"), None, "row"),
            P(("dp", "col"), "row", None),
            P(("dp", "col"), "row", None),
        ),
        out_specs=(
            P(("dp", "row", "col"), None),
            P(("dp", "row", "col"), None),
            P(),
            P(("dp", "row", "col"), None),
            P(("dp", "row", "col"), None),
            P(("dp", "row", "col"), None),
            P(("dp", "row", "col"), None, None),
            P(("dp", "row", "col"), None, None),
            P(("dp", "row", "col"), None, None),
            P(("dp", "row", "col"), None),
            P(("dp", "row", "col"), None),
            P(("dp", "row", "col"), None),
            P(("dp", "row", "col"), None),
            P(("dp", "row", "col"), None),
            P(("dp", "row", "col"), None),
            P(("dp", "col"), None, "row"),
            P(("dp", "col"), None, "row"),
            P(("dp", "col"), None, "row"),
            P(("dp", "col"), "row", None),
            P(("dp", "col"), "row", None),
            P(("dp", "col"), "row", None),
        ),
        check_vma=False,
    )
```

profile of v0, /device:TPU:0, one launch (start us, length us, event | category | flops | bytes accessed | tf_op | source)
XLA Modules:
  0.0 1048.5 jit_solution(11963525600608490308)
XLA Ops:
  15.5 43.3 %all-gather = bf16[32,24,4]{1,2,0:T(4,128)(2,1)S(1)} all-gather(bf16[1,24,4]{1,2,0:T(4,128)(2,1)S(1)} %convert_bitcast_fusion.3), channel_id=1, replica_groups=mesh['dp'=8,'row'=2,'col'=2] {'dp','row','col'}, dimensions={0}, use_global_device_ids=true | all-gather | bytes 6336 | tf_op jit(solution)/shard_map/all_gather | solution.py:98
  59.6 8.8 gather_fusion
  68.5 4.5 reduce-window.6
  73.9 8.8 scatter_custom_fusion
  82.7 9.0 scatter_custom_fusion.1
  92.3 6.9 convolution_convert_fusion
  99.2 8.8 reshape.415
  108.0 6.7 fusion.142
  114.7 4.8 copy.239
  126.9 5.2 fusion.143
  137.2 6.2 fusion.87
  152.3 9.4 gather_fusion.1
  166.0 4.5 all-to-all-start
  174.7 83.2 %all-gather.1 = bf16[32,24,16]{1,2,0:T(8,128)(2,1)S(1)} all-gather(bf16[1,24,16]{1,2,0:T(8,128)(2,1)S(1)} %convert_bitcast_fusion.2), channel_id=1, replica_groups=mesh['dp'=8,'row'=2,'col'=2] {'dp','row','col'}, dimensions={0}, use_global_device_ids=true | all-gather | bytes 25344 | tf_op jit(solution)/shard_map/all_gather | solution.py:101
  262.0 7.1 mul.523
  269.5 20.1 %gather_fusion.5 = f32[1576]{0:T(1024)S(1)} fusion(f32[788,16]{0,1:T(8,128)S(1)} %fusion.145, s32[1576]{0:T(1024)S(1)} %reshape.365), kind=kCustom, calls=%fused_computation.5 | custom fusion | bytes 25216 | tf_op jit(solution)/shard_map/jit(take_along_axis)/gather | solution.py:130
  295.2 9.4 gather_fusion.3
  308.9 13.5 %all-to-all-start.2 = ((bf16[16,1,124,768]{3,2,1,0:T(8,128)(2,1)}), bf16[16,1,124,768]{3,2,1,0:T(8,128)(2,1)}, u32[]{:S(2)}, u32[]{:S(2)}) async-start(bf16[16,1,124,768]{3,2,1,0:T(8,128)(2,1)} %bitcast.31), calls=%async_computation.2 | async-start | bytes 6291456 | tf_op jit(solution)/shard_map/all_to_all | solution.py:168
  322.4 17.4 %fusion.42 = f32[16,124,3072]{2,1,0:T(8,128)} fusion(bf16[1,768,3072]{2,1,0:T(8,128)(2,1)} %all-gather.11.cloned.1.call-done, bf16[16,1,124,768]{3,2,1,0:T(8,128)(2,1)} %all-to-all-done), kind=kOutput, calls=%fused_computation.71 | convolution fusion | flops 9361686528 | bytes 32145408 | tf_op jit(solution)/shard_map/sjcd,jdf->sjcf/dot_general | solution.py:148
  339.8 67.9 %convert_bitcast_fusion.1 = bf16[16,1,124,768]{3,2,1,0:T(8,128)(2,1)} fusion(bf16[1,3072,768]{2,1,0:T(8,128)(2,1)} %all-gather.13.cloned.1.call-done, f32[16,124,3072]{2,1,0:T(8,128)} %fusion.42), kind=kOutput, calls=%fused_computation.93 | convolution fusion | flops 9759375360 | bytes 32145408 | tf_op jit(solution)/shard_map/sjcf,jfd->sjcd/dot_general | solution.py:151
  407.8 6.0 all-to-all-start.1
  413.8 69.1 %fusion.7 = bf16[16,1,124,3072]{3,2,0,1:T(8,128)(2,1)S(1)} fusion(f32[16,124,3072]{2,1,0:T(8,128)} %fusion.42, bf16[1,3072,768]{2,1,0:T(8,128)(2,1)} %all-gather.13.cloned.1.call-done, bf16[16,1,124,768]{3,2,1,0:T(8,128)(2,1)} %all-to-all-done.2), kind=kOutput, calls=%fused_computation.18 | convolution fusion | flops 9800515584 | bytes 44335104 | tf_op jit(solution)/shard_map/sjcd,jfd->sjcf/dot_general | solution.py:169
  482.9 4.5 copy-done.83
  487.4 11.3 %convert_bitcast_fusion = bf16[16,1,124,768]{3,2,1,0:T(8,128)(2,1)} fusion(bf16[1,768,3072]{2,1,0:T(8,128)(2,1)S(1)} %copy-done.81, bf16[16,1,124,3072]{3,2,0,1:T(8,128)(2,1)S(1)} %fusion.7), kind=kOutput, calls=%fused_computation.92 | convolution fusion | flops 9363210240 | bytes 19955712 | tf_op jit(solution)/shard_map/sjcf,jdf->sjcd/dot_general | solution.py:187
  498.7 6.1 all-to-all-start.3
  506.6 4.4 reshape.316
  513.0 6.2 gather_fusion.2
  519.2 6.6 reshape.323
  525.8 13.6 %multiply_reduce_fusion.2 = (f32[788,2]{1,0:T(8,128)S(1)}, f32[788,768]{1,0:T(8,128)}) fusion(f32[788,2,768]{2,1,0:T(2,128)} %reshape.323, f32[788,768]{1,0:T(8,128)S(1)} %copy-done.15, f32[788,2]{1,0:T(8,128)S(1)} %copy-done.21), kind=kLoop, calls=%fused_computation.59 | loop fusion | flops 4234712 | bytes 9695552 | tf_op jit(solution)/shard_map/reduce_sum | solution.py:162
  539.8 24.6 %all-to-all-done.3 = bf16[16,1,124,768]{3,2,1,0:T(8,128)(2,1)} async-done(((bf16[16,1,124,768]{3,2,1,0:T(8,128)(2,1)}), bf16[16,1,124,768]{3,2,1,0:T(8,128)(2,1)}, u32[]{:S(2)}, u32[]{:S(2)}) %all-to-all-start.3) | async-done | bytes 3047456 | tf_op jit(solution)/shard_map/all_to_all | solution.py:188
  570.7 6.2 gather_fusion.4
  576.9 6.6 reshape.324
  583.6 9.7 reduce_sum.286
  603.8 15.3 %fusion.44 = bf16[1,768,3072]{2,1,0:T(8,128)(2,1)} fusion(bf16[16,1,124,3072]{3,2,0,1:T(8,128)(2,1)} %copy-done.83, bf16[16,1,124,768]{3,2,1,0:T(8,128)(2,1)} %all-to-all-done), kind=kOutput, calls=%fused_computation.75 | convolution fusion | flops 9364045824 | bytes 19955712 | tf_op jit(solution)/shard_map/sjcd,sjcf->jdf/dot_general | solution.py:173
  619.3 64.7 %fusion.47 = bf16[1,3072,768]{2,1,0:T(8,128)(2,1)} fusion(bf16[16,1,124,768]{3,2,1,0:T(8,128)(2,1)} %all-to-all-done.2, f32[16,124,3072]{2,1,0:T(8,128)} %fusion.42), kind=kOutput, calls=%fused_computation.76 | convolution fusion | flops 9760210944 | bytes 32145408 | tf_op jit(solution)/shard_map/sjcf,sjcd->jfd/dot_general | solution.py:176
  696.8 7.2 fusion.92
  711.3 10.6 %multiply_reduce_fusion = (f32[4,12,197]{2,1,0:T(8,128)S(1)}, f32[4,12,197,197]{2,3,1,0:T(8,128)}) fusion(f32[4,12,197,197]{2,3,1,0:T(8,128)} %get-tuple-element.64, f32[4,12,197]{2,1,0:T(8,128)S(1)} %copy-done.30, bf16[4,197,12,64]{1,3,2,0:T(8,128)(2,1)} %copy.205, bf16[4,197,1,12,64]{1,4,3,0,2:T(8,128)(2,1)} %copy-done.22), kind=kOutput, calls=%fused_computation.42 | convolution fusion | flops 244021536 | bytes 17399040 | tf_op jit(solution)/shard_map/ishd,ijhd->ihsj/dot_general | solution.py:210
  721.9 11.0 %multiply_convert_fusion = bf16[4,12,197,197]{2,3,1,0:T(8,128)(2,1)} fusion(f32[4,12,197,197]{2,3,1,0:T(8,128)} %get-tuple-element.69, f32[4,12,197]{2,1,0:T(8,128)S(1)} %get-tuple-element.68, f32[4,12,197,197]{2,3,1,0:T(8,128)} %get-tuple-element.64, f32[4,12,197]{2,1,0:T(8,128)S(1)} %copy-done.30), kind=kLoop, calls=%fused_computation.41 | loop fusion | flops 7451328 | bytes 18703968 | tf_op jit(solution)/shard_map/convert_element_type | solution.py:218
  741.0 5.2 reshape.409
  746.3 4.6 fusion.95
  750.9 4.5 copy.224
  763.3 6.3 fusion.105
  769.6 6.4 fusion.66
  779.2 51.7 %all-reduce.7 = (f32[768,4]{0,1:T(4,128)S(1)}, f32[768,16]{0,1:T(8,128)S(1)}) all-reduce(f32[768,4]{0,1:T(4,128)S(1)} %pad_maximum_fusion, f32[768,16]{0,1:T(8,128)S(1)} %fusion.146), channel_id=2, replica_groups=mesh['dp'=8,'row'=2,'col'=2] {'dp','row','col'}, use_global_device_ids=true, to_apply=%region_27.28.clone | all-reduce | flops 15360 | bytes 122880
  842.5 122.4 %reduce-scatter.7.cloned.1.call-done = f32[24,3,768]{2,0,1:T(8,128)} async-done(((f32[768,3,768]{2,0,1:T(8,128)}), f32[24,3,768]{2,0,1:T(8,128)}) %reduce-scatter.7.cloned.1.call-update) | async-done | bytes 221200 | tf_op jit(solution)/shard_map/reduce_scatter | solution.py:239
  974.5 40.0 %psum.7 = f32[]{:T(128)} all-reduce(f32[]{:T(128)S(6)} %add.251), channel_id=1, replica_groups=mesh['dp'=8,'row'=2,'col'=2] {'dp','row','col'}, use_global_device_ids=true, to_apply=%region_39.40 | all-reduce | flops 1 | bytes 8 | tf_op jit(solution)/shard_map/psum | solution.py:251
  1016.7 11.7 %multiply_subtract_fusion = (f32[1,1536,768]{2,1,0:T(8,128)}, f32[1,1536,768]{2,1,0:T(8,128)}, f32[1,1536,768]{2,1,0:T(8,128)}) fusion(f32[1,1536,768]{2,1,0:T(8,128)} %param.31, f32[]{:T(128)S(6)} %min.3, bf16[1,1536,768]{2,1,0:T(8,128)(2,1)} %reduce-scatter.13.cloned.1.call-done, f32[1,1536,768]{2,1,0:T(8,128)} %param.43, f32[1,1536,768]{2,1,0:T(8,128)} %param.42), kind=kLoop, calls=%fused_computation.73 | loop fusion | flops 20054016 | bytes 30670852 | tf_op jit(solution)/shard_map/sub | solution.py:57
  1029.5 9.0 multiply_subtract_fusion.1
  (302 shorter events, 136.1 us)
Async XLA Ops:
  7.2 85.1 %all-gather.7.cloned.1.call-start = ((), (), s32[]{:S(2)}) async-start(), calls=%async_computation.8 | async-start | bytes 3649536 | tf_op jit(solution)/shard_map/all_gather | solution.py:99
  8.9 138.4 %all-gather.9.cloned.1.call-start = ((), (), s32[]{:S(2)}) async-start(), calls=%async_computation.9 | async-start | bytes 1216512 | tf_op jit(solution)/shard_map/all_gather | solution.py:100
  10.5 48.7 %copy-start.39 = (s32[788,2]{0,1:T(2,128)S(1)}, s32[788,2]{0,1:T(2,128)}, u32[]{:S(2)}) copy-start(s32[788,2]{0,1:T(2,128)} %param.24) | copy-start | bytes 18916
  10.5 312.0 %all-gather.11.cloned.1.call-start = ((), (), s32[]{:S(2)}) async-start(), calls=%async_computation.10 | async-start | bytes 7077888 | tf_op jit(solution)/shard_map/all_gather | solution.py:145
  14.6 45.0 %copy-start.76 = (s32[1,1576]{1,0:T(1,128)S(1)}, s32[1,1576]{1,0:T(1,128)}, u32[]{:S(2)}) copy-start(s32[1,1576]{1,0:T(1,128)} %param.25) | copy-start | bytes 18916
  14.9 77.4 %copy-start.47 = (f32[788]{0:T(1024)}, f32[788]{0:T(1024)S(1)}, u32[]{:S(2)}) copy-start(f32[788]{0:T(1024)S(1)} %broadcast_multiply_fusion.1) | copy-start | bytes 9460
  15.5 43.5 %copy-start.59 = (f32[788]{0:T(1024)}, f32[788]{0:T(1024)S(1)}, u32[]{:S(2)}) copy-start(f32[788]{0:T(1024)S(1)} %fusion.65) | copy-start | bytes 9460
  15.5 76.8 %copy-start.57 = (f32[788]{0:T(1024)}, f32[788]{0:T(1024)S(1)}, u32[]{:S(2)}) copy-start(f32[788]{0:T(1024)S(1)} %fusion.125) | copy-start | bytes 9460
  59.1 33.2 %copy-start.55 = (f32[768]{0:T(1024)}, f32[768]{0:T(1024)S(1)}, u32[]{:S(2)}) copy-start(f32[768]{0:T(1024)S(1)} %get-tuple-element.32) | copy-start | bytes 9220
  59.1 33.2 %copy-start.77 = (f32[768]{0:T(1024)}, f32[768]{0:T(1024)S(1)}, u32[]{:S(2)}) copy-start(f32[768]{0:T(1024)S(1)} %get-tuple-element.31) | copy-start | bytes 9220
  59.2 91.7 %copy-start.51 = (f32[768]{0:T(1024)}, f32[768]{0:T(1024)S(1)}, u32[]{:S(2)}) copy-start(f32[768]{0:T(1024)S(1)} %get-tuple-element.29) | copy-start | bytes 9220
  82.7 16.5 %copy-start.66 = (s32[1576]{0:T(1024)}, s32[1576]{0:T(1024)S(1)}, u32[]{:S(2)}) copy-start(s32[1576]{0:T(1024)S(1)} %compare_select_fusion.3) | copy-start | bytes 18916
  132.1 11.4 %copy-start.29 = (f32[4,12,197]{2,1,0:T(8,128)}, f32[4,12,197]{2,1,0:T(8,128)S(1)}, u32[]{:S(2)}) copy-start(f32[4,12,197]{2,1,0:T(8,128)S(1)} %get-tuple-element.63) | copy-start | bytes 113476
  150.8 10.9 %copy-start.61 = (f32[788]{0:T(1024)}, f32[788]{0:T(1024)S(1)}, u32[]{:S(2)}) copy-start(f32[788]{0:T(1024)S(1)} %multiply_reduce_fusion.6) | copy-start | bytes 9460
  150.8 10.8 %copy-start.53 = (f32[788]{0:T(1024)}, f32[788]{0:T(1024)S(1)}, u32[]{:S(2)}) copy-start(f32[788]{0:T(1024)S(1)} %fusion.126) | copy-start | bytes 9460
  152.2 116.9 %copy-start.4 = (bf16[788,768]{1,0:T(8,128)(2,1)}, bf16[788,768]{1,0:T(8,128)(2,1)S(1)}, u32[]{:S(2)}) copy-start(bf16[788,768]{1,0:T(8,128)(2,1)S(1)} %add_convert_fusion.1) | copy-start | bytes 3631108
  166.0 142.9 %all-to-all-start = ((bf16[16,1,124,768]{3,2,1,0:T(8,128)(2,1)}), bf16[16,1,124,768]{3,2,1,0:T(8,128)(2,1)}, u32[]{:S(2)}, u32[]{:S(2)}) async-start(bf16[16,1,124,768]{3,2,1,0:T(8,128)(2,1)} %bitcast.274), calls=%async_computation | async-start | bytes 6291456 | tf_op jit(solution)/shard_map/all_to_all | solution.py:141
  170.5 88.1 %copy-start.9 = (bf16[788,768]{1,0:T(8,128)(2,1)S(1)}, bf16[788,768]{1,0:T(8,128)(2,1)}, u32[]{:S(2)}) copy-start(bf16[788,768]{1,0:T(8,128)(2,1)} %param.23) | copy-start | bytes 3631108
  170.5 169.3 %all-gather.13.cloned.1.call-start = ((), (), s32[]{:S(2)}) async-start(), calls=%async_computation.11 | async-start | bytes 7077888 | tf_op jit(solution)/shard_map/all_gather | solution.py:146
  258.1 10.9 %copy-start.33 = (bf16[768,16]{0,1:T(8,128)(2,1)}, bf16[768,16]{0,1:T(8,128)(2,1)S(1)}, u32[]{:S(2)}) copy-start(bf16[768,16]{0,1:T(8,128)(2,1)S(1)} %reshape.400) | copy-start | bytes 73732
  308.9 98.9 %all-to-all-start.2 = ((bf16[16,1,124,768]{3,2,1,0:T(8,128)(2,1)}), bf16[16,1,124,768]{3,2,1,0:T(8,128)(2,1)}, u32[]{:S(2)}, u32[]{:S(2)}) async-start(bf16[16,1,124,768]{3,2,1,0:T(8,128)(2,1)} %bitcast.31), calls=%async_computation.2 | async-start | bytes 6291456 | tf_op jit(solution)/shard_map/all_to_all | solution.py:168
  407.8 91.0 %all-to-all-start.1 = ((bf16[16,1,124,768]{3,2,1,0:T(8,128)(2,1)}), bf16[16,1,124,768]{3,2,1,0:T(8,128)(2,1)}, u32[]{:S(2)}, u32[]{:S(2)}) async-start(bf16[16,1,124,768]{3,2,1,0:T(8,128)(2,1)} %convert_bitcast_fusion.1), calls=%async_computation.1 | async-start | bytes 6291456 | tf_op jit(solution)/shard_map/all_to_all | solution.py:152
  413.8 73.6 %copy-start.81 = (bf16[1,768,3072]{2,1,0:T(8,128)(2,1)S(1)}, bf16[1,768,3072]{2,1,0:T(8,128)(2,1)}, u32[]{:S(2)}) copy-start(bf16[1,768,3072]{2,1,0:T(8,128)(2,1)} %all-gather.11.cloned.1.call-done) | copy-start | bytes 14155780
  498.7 65.6 %all-to-all-start.3 = ((bf16[16,1,124,768]{3,2,1,0:T(8,128)(2,1)}), bf16[16,1,124,768]{3,2,1,0:T(8,128)(2,1)}, u32[]{:S(2)}, u32[]{:S(2)}) async-start(bf16[16,1,124,768]{3,2,1,0:T(8,128)(2,1)} %convert_bitcast_fusion), calls=%async_computation.3 | async-start | bytes 6291456 | tf_op jit(solution)/shard_map/all_to_all | solution.py:188
  504.9 327.3 %reduce-scatter.9.cloned.1.call-start = ((), (), s32[]{:S(2)}) async-start(), calls=%async_computation.13 | async-start | bytes 2433024 | tf_op jit(solution)/shard_map/reduce_scatter | solution.py:240
  525.8 13.8 %copy-start.38 = (f32[788,2]{0,1:T(2,128)S(1)}, f32[788,2]{0,1:T(2,128)}, u32[]{:S(2)}) copy-start(f32[788,2]{0,1:T(2,128)} %copy-done.37) | copy-start | bytes 18916
  525.8 13.8 %copy-start.42 = (f32[788]{0:T(1024)S(1)}, f32[788]{0:T(1024)}, u32[]{:S(2)}) copy-start(f32[788]{0:T(1024)} %copy-done.41) | copy-start | bytes 9460
  525.8 13.9 %copy-start.50 = (f32[788]{0:T(1024)S(1)}, f32[788]{0:T(1024)}, u32[]{:S(2)}) copy-start(f32[788]{0:T(1024)} %copy-done.49) | copy-start | bytes 9460
  525.8 13.9 %copy-start.40 = (s32[788,2]{0,1:T(2,128)S(1)}, s32[788,2]{0,1:T(2,128)}, u32[]{:S(2)}) copy-start(s32[788,2]{0,1:T(2,128)} %param.24) | copy-start | bytes 18916
  539.7 53.5 %copy-start.31 = (bf16[788,16]{0,1:T(8,128)(2,1)}, bf16[788,16]{0,1:T(8,128)(2,1)S(1)}, u32[]{:S(2)}) copy-start(bf16[788,16]{0,1:T(8,128)(2,1)S(1)} %select_reduce_fusion) | copy-start | bytes 75652
  603.8 229.9 %reduce-scatter.11.cloned.1.call-start = ((), (), s32[]{:S(2)}) async-start(), calls=%async_computation.14 | async-start | bytes 7077888 | tf_op jit(solution)/shard_map/reduce_scatter | solution.py:180
  619.2 219.8 %reduce-scatter.13.cloned.1.call-start = ((), (), s32[]{:S(2)}) async-start(), calls=%async_computation.15 | async-start | bytes 7077888 | tf_op jit(solution)/shard_map/reduce_scatter | solution.py:183
  683.9 280.9 %reduce-scatter.7.cloned.1.call-start = ((), (), s32[]{:S(2)}) async-start(), calls=%async_computation.12 | async-start | bytes 7299072 | tf_op jit(solution)/shard_map/reduce_scatter | solution.py:239
  721.9 11.0 %copy-start.8 = (bf16[4,197,1,12,64]{1,4,3,0,2:T(8,128)(2,1)S(1)}, bf16[4,197,1,12,64]{1,4,3,0,2:T(8,128)(2,1)}, u32[]{:S(2)}) copy-start(bf16[4,197,1,12,64]{1,4,3,0,2:T(8,128)(2,1)} %copy.239) | copy-start | bytes 3631108
  777.5 192.9 %copy-start.13 = (bf16[788,768]{1,0:T(8,128)(2,1)S(1)}, bf16[788,768]{1,0:T(8,128)(2,1)}, u32[]{:S(2)}) copy-start(bf16[788,768]{1,0:T(8,128)(2,1)} %param.23) | copy-start | bytes 3631108
  970.4 44.9 %copy-start.65 = (f32[24,16]{0,1:T(8,128)S(1)}, f32[24,16]{0,1:T(8,128)}, u32[]{:S(2)}) copy-start(f32[24,16]{0,1:T(8,128)} %param.29) | copy-start | bytes 4612
  970.4 44.9 %copy-start.72 = (f32[24,16]{0,1:T(8,128)S(1)}, f32[24,16]{0,1:T(8,128)}, u32[]{:S(2)}) copy-start(f32[24,16]{0,1:T(8,128)} %param.39) | copy-start | bytes 4612
  970.4 44.9 %copy-start.73 = (f32[24,16]{0,1:T(8,128)S(1)}, f32[24,16]{0,1:T(8,128)}, u32[]{:S(2)}) copy-start(f32[24,16]{0,1:T(8,128)} %param.38) | copy-start | bytes 4612
  970.4 45.6 %copy-start.75 = (f32[24,4]{0,1:T(4,128)S(1)}, f32[24,4]{0,1:T(4,128)}, u32[]{:S(2)}) copy-start(f32[24,4]{0,1:T(4,128)} %param.26) | copy-start | bytes 1156
  970.4 45.6 %copy-start.79 = (f32[24,4]{0,1:T(4,128)S(1)}, f32[24,4]{0,1:T(4,128)}, u32[]{:S(2)}) copy-start(f32[24,4]{0,1:T(4,128)} %param.33) | copy-start | bytes 1156
  970.4 45.6 %copy-start.80 = (f32[24,4]{0,1:T(4,128)S(1)}, f32[24,4]{0,1:T(4,128)}, u32[]{:S(2)}) copy-start(f32[24,4]{0,1:T(4,128)} %param.32) | copy-start | bytes 1156
  970.4 58.0 %slice-start = ((s8[4718592]{0:T(1024)(128)(4,1)}), s8[524288]{0:T(1024)(128)(4,1)S(1)}, s32[]{:S(2)}) async-start(s8[4718592]{0:T(1024)(128)(4,1)} %bitcast.272), calls=%async_computation.16 | async-start | bytes 1048576
  1016.7 11.7 %slice-start.1 = ((s8[4718592]{0:T(1024)(128)(4,1)}), s8[4194304]{0:T(1024)(128)(4,1)S(1)}, s32[]{:S(2)}) async-start(s8[4718592]{0:T(1024)(128)(4,1)} %bitcast.272), calls=%async_computation.17 | async-start | bytes 8388608
  1016.7 12.8 %copy-start.18 = (bf16[1,768,1536]{2,1,0:T(8,128)(2,1)S(1)}, bf16[1,768,1536]{2,1,0:T(8,128)(2,1)}, u32[]{:S(2)}) copy-start(bf16[1,768,1536]{2,1,0:T(8,128)(2,1)} %reduce-scatter.11.cloned.1.call-done) | copy-start | bytes 7077892
  1029.5 9.8 copy-start.24
  1029.5 9.8 copy-start.25
  1029.5 9.8 copy-start.35
  1029.5 9.8 copy-start.36
  (50 other events, 254.8 us)
Sparse Core Ops, SparseCore 0:
  11.4 62.8 all-gather.6
  77.9 52.8 all-gather.8
  132.9 61.7 all-gather.10
  196.7 63.8 all-gather.12
  603.9 108.8 reduce-scatter.8
  715.6 59.0 reduce-scatter.10
  777.6 61.3 reduce-scatter.12
  845.6 119.2 reduce-scatter.6
where the time goes:
time: 1060 us; the launch traced here: 1050 us
  matrix products  316 us (30%)
  blocking collectives  218 us (21%)
  local copies, waits for them, and re-layouts  208 us (20%)
  waiting for transfers between devices  149 us (14%)
  other arithmetic  105 us (10%)
  starting transfers between devices  30.4 us (3%)
  between operations  21.5 us (2%)
    reduce_scatter x1, waiting for transfers between devices, on_device(): lax.psum_scatter(qkv_grad, ('dp', 'row', 'col'), scatter_dimension=0, til...  122 us
    all_gather x1, blocking collectives, on_device(): lax.all_gather(router_weight.astype(low_type), ('dp', 'row', 'col'), axis...  83.2 us
    dot_general x1, matrix products, on_device(): jnp.einsum('sjcd,jfd->sjcf', grad_arrived, outer_full, preferred_element_...  69.1 us
    dot_general x1, matrix products, on_device(): jnp.einsum('sjcf,jfd->sjcd', hidden, outer_full, preferred_element_type=f...  67.9 us
    dot_general x1, matrix products, on_device(): jnp.einsum('sjcf,sjcd->jfd', hidden, grad_arrived, preferred_element_type...  64.7 us
    unnamed x1, blocking collectives  51.7 us
    all_gather x1, blocking collectives, on_device(): lax.all_gather(norm_params.astype(low_type), ('dp', 'row', 'col'), axis=0...  43.3 us
    psum x1, blocking collectives, on_device(): square_sum = lax.psum(local_square, ('dp', 'row', 'col'))  40 us
  transfers between devices with their start and end apart: 12, of which 3 were waited for; matrix products, arithmetic and copies ran while one was open for 52% of the time, Pallas kernels for 0%

commit v1 on v0

v1 whole, which is shorter than its diff:
```python
import functools

import jax
import jax.numpy as jnp
from jax import lax
from jax.experimental import pallas as pl
from jax.experimental.pallas import tpu as pltpu
from jax.sharding import PartitionSpec as P

HEADS = 12
HEAD = 64
SEQ = 197
STEP = 10

NORM_EPS = 1e-06
CLIP_NORM = 1.0
BETA_ONE = 0.9
BETA_TWO = 0.999
ADAM_EPS = 1e-08
RATE_MATRIX = 0.08
RATE_NORM = 0.4
DECAY_MATRIX = 0.1

LANES = 128
MIB = 1024 * 1024
SMALL_COST = pl.CostEstimate(flops=1024, bytes_accessed=1024, transcendentals=0)
ALL = ("dp", "row", "col")
GROUP = ("dp", "col")
BF = jnp.bfloat16
F32 = jnp.float32

ERFC_P = 0.39
LOG2_E = 1.4426950408889634
ERFC_C = (
    0.23532534336933997,
    0.09138763496502661,
    0.649561341403834,
    -0.6354026835533981,
    0.8866658487971544,
    -0.2275374866853928,
)


def round_up(value, unit):
    return -(-value // unit) * unit


def dot_nn(a, b):
    return lax.dot_general(a, b, (((1,), (0,)), ((), ())), preferred_element_type=F32)


def dot_nt(a, b):
    return lax.dot_general(a, b, (((1,), (1,)), ((), ())), preferred_element_type=F32)


def dot_tn(a, b):
    return lax.dot_general(a, b, (((0,), (0,)), ((), ())), preferred_element_type=F32)


def iota(shape, dim):
    return lax.broadcasted_iota(jnp.int32, shape, dim)


def ones_where(cond):
    return jnp.where(cond, 1.0, 0.0)


def split_three(value):
    high = value.astype(BF)
    rest = value - high.astype(F32)
    middle = rest.astype(BF)
    low = (rest - middle.astype(F32)).astype(BF)
    return high, middle, low


def kernel_params(mebibytes):
    return pltpu.CompilerParams(vmem_limit_bytes=mebibytes * MIB)


def norm_parts(rows):
    mean_val = jnp.mean(rows, axis=-1, keepdims=True)
    centred = rows - mean_val
    spread_val = jnp.mean(centred * centred, axis=-1, keepdims=True)
    inv = lax.rsqrt(spread_val + NORM_EPS)
    return centred * inv, inv


def norm_back(upstream, gain, normal, inv):
    scaled = upstream * gain
    return inv * (
        scaled
        - jnp.mean(scaled, axis=-1, keepdims=True)
        - normal * jnp.mean(scaled * normal, axis=-1, keepdims=True)
    )


class Sizes:
    def __init__(self, tok_count, width, choose, experts):
        self.tok = tok_count
        self.width = width
        self.choose = choose
        self.experts = experts
        self.pairs = tok_count * choose
        self.cap = max(2, (5 * self.pairs + 4 * experts - 1) // (4 * experts))
        half = 16
        while 2 * (half - 1) < self.cap:
            half *= 2
        self.half = half
        self.chunk = experts * half
        self.images = tok_count // SEQ
        self.seq_pad = round_up(SEQ, 32)
        self.rows = self.images * self.seq_pad
        self.rank = round_up(self.pairs, 256)
        self.packed = round_up(4 * width + experts + 4, LANES)
        self.part_one = 2 * width
        self.part_two = self.packed - self.part_one


def slots_kernel(sz, order_ref, routes_ref, dy_ref, slot_ref, send_ref, hot_ref):
    rows, rank, experts, half, chunk = sz.rows, sz.rank, sz.experts, sz.half, sz.chunk
    order = order_ref[...]
    ranked = jnp.zeros((experts, rank), F32)
    for start in range(0, sz.choose * rows, 256):
        size = min(256, sz.choose * rows - start)
        hit = ones_where(order == iota((size, rank), 0) + start).astype(BF)
        hot_ref[start : start + size, :] = hit
        kind = ones_where(
            routes_ref[0:1, start : start + size] == iota((experts, size), 0)
        ).astype(BF)
        ranked += dot_nn(kind, hit)
    ranked_low = ranked.astype(BF)
    before = jnp.zeros((experts, rank), F32)
    for start in range(0, rank, 256):
        earlier = ones_where(iota((256, rank), 0) + start < iota((256, rank), 1)).astype(BF)
        before += dot_nn(ranked_low[:, start : start + 256], earlier)
    position = jnp.sum(before * ranked, axis=0, keepdims=True)
    named = jnp.sum(ranked * iota((experts, rank), 0).astype(F32), axis=0, keepdims=True)
    real = jnp.sum(ranked, axis=0, keepdims=True)
    kept = real * ones_where(position < sz.cap)
    second = ones_where(position >= half - 1)
    row_in = position + 1.0 - second * (half - 1)
    row_in = jnp.where(kept > 0.5, row_in, 0.0)
    part = iota((16, rank), 0)
    codes = jnp.where(
        part == 0, named, jnp.where(part == 1, row_in, jnp.where(part == 2, second, kept))
    )
    codes = jnp.where(part < 4, codes, 0.0).astype(BF)
    wide = iota((LANES, rows), 0)
    table = jnp.full((LANES, rows), -1.0, F32)
    for k in range(sz.choose):
        route = routes_ref[0:1, k * rows : (k + 1) * rows].astype(F32)
        table = jnp.where(wide == sz.choose + k, route, table)
    for k in range(sz.choose):
        back = dot_nt(codes, hot_ref[k * rows : (k + 1) * rows, :])
        slot = jnp.where(
            back[3:4] > 0.5, back[2:3] * chunk + back[0:1] * half + back[1:2], -1.0
        )
        table = jnp.where(wide == k, slot, table)
    slot_ref[...] = table[0:8].astype(jnp.int32)
    slots = slot_ref[...]
    block = min(256, chunk)
    dy = dy_ref[...]
    for c in range(2):
        for start in range(0, chunk, block):
            ids = iota((block, rows), 0) + (c * chunk + start)
            pick = ids == slots[0:1]
            for k in range(1, sz.choose):
                pick = pick | (ids == slots[k : k + 1])
            moved = dot_nn(ones_where(pick).astype(BF), dy).astype(BF)
            send_ref[start // half : (start + block) // half, c * half : (c + 1) * half] = (
                moved.reshape(block // half, half, sz.width)
            )


def call_slots(sz, order, routes_row, dy):
    return pl.pallas_call(
        functools.partial(slots_kernel, sz),
        out_shape=(
            jax.ShapeDtypeStruct((8, sz.rows), jnp.int32),
            jax.ShapeDtypeStruct((sz.experts, 2 * sz.half, sz.width), BF),
        ),
        scratch_shapes=[pltpu.VMEM((sz.choose * sz.rows, sz.rank), BF)],
        compiler_params=kernel_params(56),
        cost_estimate=SMALL_COST,
        name="slots",
    )(order, routes_row, dy)


def attend_kernel(
    sz,
    tok_ref,
    w_one_ref,
    w_two_ref,
    routes_ref,
    slot_ref,
    qkv_ref,
    lse_ref,
    mixed_ref,
    after_ref,
    normed_ref,
    gate_ref,
    gate_col_ref,
    send_one_ref,
    send_two_ref,
    normed_all,
    tail_t,
):
    width, seq, rows = sz.width, sz.seq_pad, sz.rows
    step = pl.program_id(0)

    @pl.when(step == 0)
    def _():
        tail_t[...] = w_two_ref[:, 2 * width :].astype(F32).T

    first = sz.experts
    gain_one, bias_one = tail_t[first : first + 1], tail_t[first + 1 : first + 2]
    gain_two, bias_two = tail_t[first + 2 : first + 3], tail_t[first + 3 : first + 4]
    tok = tok_ref[...].astype(F32)
    normal, _ = norm_parts(tok)
    normed = (normal * gain_one + bias_one).astype(BF)
    qkv_ref[:, : 2 * width] = dot_nn(normed, w_one_ref[...]).astype(BF)
    qkv_ref[:, 2 * width :] = dot_nn(normed, w_two_ref[:, :width]).astype(BF)
    lane = iota((seq, LANES), 1)
    key_ok = iota((seq, seq), 0) < SEQ
    pair_lane = iota((1, LANES), 1) // HEAD
    for j in range(HEADS // 2):
        at = j * LANES
        q = qkv_ref[:, at : at + LANES]
        key = qkv_ref[:, width + at : width + at + LANES]
        val = qkv_ref[:, 2 * width + at : 2 * width + at + LANES]
        outs = []
        for a in range(2):
            own = jnp.where(pair_lane == a, HEAD**-0.5, 0.0).astype(BF)
            scores = jnp.where(key_ok, dot_nt(key, q * own), -1e30)
            top = jnp.max(scores, axis=0, keepdims=True)
            raised = jnp.exp(scores - top)
            total = jnp.sum(raised, axis=0, keepdims=True)
            probs = (raised * (1.0 / total)).astype(BF)
            outs.append(dot_tn(probs, val))
            lse_ref[2 * j + a : 2 * j + a + 1, :] = top + jnp.log(total)
        mixed_ref[:, at : at + LANES] = jnp.where(lane < HEAD, outs[0], outs[1]).astype(BF)
    after = tok + dot_nt(mixed_ref[...], w_two_ref[:, width : 2 * width])
    after_ref[...] = after
    normal, _ = norm_parts(after)
    normed_two = (normal * gain_two + bias_two).astype(BF)
    normed_ref[...] = normed_two
    normed_all[pl.ds(step * seq, seq), :] = normed_two

    @pl.when(step == sz.images - 1)
    def _():
        normed_two = normed_all[...]
        logits = dot_nt(tail_t[...].astype(BF), normed_two)
        kinds = iota((LANES, rows), 0)
        chosen = [
            jnp.sum(jnp.where(kinds == routes_ref[k : k + 1], logits, 0.0), axis=0, keepdims=True)
            for k in range(sz.choose)
        ]
        top = functools.reduce(jnp.maximum, chosen)
        raised = [jnp.exp(c - top) for c in chosen]
        total = functools.reduce(jnp.add, raised)
        gates = [r / total for r in raised]
        wide = jnp.zeros((LANES, rows), F32)
        for k in range(sz.choose):
            wide = jnp.where(kinds == k, gates[k], wide)
        gate_ref[...] = wide[0:8]
        gate_col_ref[...] = wide.T
        half, chunk = sz.half, sz.chunk
        part = iota((16, rows), 0)
        coded = []
        for k in range(sz.choose):
            pieces = split_three(gates[k])
            table = jnp.zeros((16, rows), F32)
            for m in range(3):
                table = jnp.where(part == m, pieces[m].astype(F32), table)
            coded.append(table.astype(BF))
        block = min(256, chunk)
        for c, out_ref in enumerate((send_one_ref, send_two_ref)):
            for start in range(0, chunk, block):
                ids = iota((block, rows), 0) + (c * chunk + start)
                picks = [
                    ones_where(ids == slot_ref[k : k + 1]).astype(BF) for k in range(sz.choose)
                ]
                moved = dot_nn(functools.reduce(jnp.add, picks), normed_two)
                meta = functools.reduce(
                    jnp.add, [dot_nt(coded[k], picks[k]) for k in range(sz.choose)]
                )
                for e in range(block // half):
                    base, shift = (e * half) // LANES * LANES, (e * half) % LANES
                    near = meta[0:8, base : base + LANES] if block >= LANES else meta[0:8]
                    if shift:
                        near = pltpu.roll(near, LANES - shift, axis=1)
                    line = jnp.concatenate(
                        [near[0:1], near[1:2], near[2:3], jnp.zeros((1, width - 3 * LANES), F32)],
                        axis=1,
                    )
                    body = moved[e * half : (e + 1) * half]
                    body = jnp.where(iota((half, width), 0) == 0, line, body)
                    at = start + e * half
                    out_ref[at : at + half, :] = body.astype(BF)


def call_attend(sz, tok, packed, routes_row, slots):
    images, seq, width, rows = sz.images, sz.seq_pad, sz.width, sz.rows
    per_image = lambda size: pl.BlockSpec((None, seq, size), lambda i: (i, 0, 0))
    lse_spec = pl.BlockSpec((None, 16, seq), lambda i: (i, 0, 0))
    whole = lambda *shape: pl.BlockSpec(shape, lambda i: (0,) * len(shape))
    return pl.pallas_call(
        functools.partial(attend_kernel, sz),
        grid=(images,),
        in_specs=[
            per_image(width),
            whole(width, sz.part_one),
            whole(width, sz.part_two),
            whole(8, rows),
            whole(8, rows),
        ],
        out_specs=(
            per_image(3 * width),
            lse_spec,
            per_image(width),
            per_image(width),
            per_image(width),
            whole(8, rows),
            whole(rows, LANES),
            whole(sz.chunk, width),
            whole(sz.chunk, width),
        ),
        out_shape=(
            jax.ShapeDtypeStruct((images, seq, 3 * width), BF),
            jax.ShapeDtypeStruct((images, 16, seq), F32),
            jax.ShapeDtypeStruct((images, seq, width), BF),
            jax.ShapeDtypeStruct((images, seq, width), F32),
            jax.ShapeDtypeStruct((images, seq, width), BF),
            jax.ShapeDtypeStruct((8, rows), F32),
            jax.ShapeDtypeStruct((rows, LANES), F32),
            jax.ShapeDtypeStruct((sz.chunk, width), BF),
            jax.ShapeDtypeStruct((sz.chunk, width), BF),
        ),
        scratch_shapes=[pltpu.VMEM((rows, width), BF), pltpu.VMEM((LANES, width), F32)],
        compiler_params=kernel_params(56),
        cost_estimate=SMALL_COST,
        name="attend",
    )(tok, *packed, routes_row, slots)


def own_copies(per_ring, block, in_own, out_own, w_in, w_out):
    copies = []
    for j in range(per_ring):
        cols = slice(j * block, (j + 1) * block)
        copies.append((j, in_own.at[:, cols], w_in.at[j]))
        copies.append((j, out_own.at[cols, :], w_out.at[j]))
    return copies


def far_copies(ring, per_ring, block, first_step, in_far, out_far, w_in, w_out):
    copies = []
    for r in range(ring - 1):
        for j in range(per_ring):
            step, start = first_step + per_ring * r + j, j * block
            at = 0
            for piece in in_far:
                rows = slice(at, at + piece.shape[1])
                copies.append(
                    (step, piece.at[r, :, start : start + block], w_in.at[step, rows, :])
                )
                at += piece.shape[1]
            at = 0
            for piece in out_far:
                first, last = max(at, start), min(at + piece.shape[1], start + block)
                if first < last:
                    copies.append(
                        (
                            step,
                            piece.at[r, first - at : last - at, :],
                            w_out.at[step, first - start : last - start, :],
                        )
                    )
                at += piece.shape[1]
    return copies


def expert_kernel(sz, ring, per_ring, own, far, extra, in_count, out_count, *refs):
    refs = list(refs)
    take = lambda count: [refs.pop(0) for _ in range(count)]
    x_ref, dy_ref = take(2)
    in_own, out_own = take(2) if own else (None, None)
    in_far, out_far = take(in_count if far else 0), take(out_count if far else 0)
    if not own:
        grad_res, res_before, back_before = take(3)
    take(extra)
    hidden_ref, inner_ref = take(2)
    if own:
        grad_res = take(1)[0]
    if far:
        res_ref, back_ref = take(2)
    res_sum, back_sum = take(2)
    acts, hids = take(2), take(2)
    w_in, w_out, sems = take(3)
    steps = w_in.shape[0]
    half, width, experts = sz.half, sz.width, sz.experts
    step = pl.program_id(0)
    diag = iota((half, LANES), 0) == iota((half, LANES), 1)
    block = w_in.shape[2]
    wanted = own_copies(per_ring, block, in_own, out_own, w_in, w_out) if own else []
    if far:
        first_step = per_ring if own else 0
        wanted += far_copies(ring, per_ring, block, first_step, in_far, out_far, w_in, w_out)
    copies = [
        (at, pltpu.make_async_copy(source, target, sems.at[n]))
        for n, (at, source, target) in enumerate(wanted)
    ]

    @pl.when(step == 0)
    def _():
        for _at, copy in copies:
            copy.start()
        if not own:
            res_sum[...] = res_before[...]
            back_sum[...] = back_before[...]
            return
        for e in range(experts):
            at = e * half
            line = x_ref[at : at + 16, 0 : 3 * LANES].astype(F32)[0:1]
            gate = line[:, 0:LANES] + line[:, LANES : 2 * LANES] + line[:, 2 * LANES :]
            gate = jnp.sum(jnp.where(diag, gate, 0.0), axis=1, keepdims=True)
            grad_res[at : at + half, :] = (gate * dy_ref[e].astype(F32)).astype(BF)
        res_sum[...] = jnp.zeros_like(res_sum)
        back_sum[...] = jnp.zeros_like(back_sum)

    for at in range(steps):

        @pl.when(step == at)
        def _(at=at):
            for when, copy in copies:
                if when == at:
                    copy.wait()

    def work():
        chunk = x_ref.shape[0]
        in_ref, out_ref = w_in.at[step], w_out.at[step]
        tile = 256 if block % 256 == 0 else 128
        count = block // tile
        pieces = [slice(n * tile, (n + 1) * tile) for n in range(count)]
        spans = [slice(at, at + min(256, chunk)) for at in range(0, chunk, 256)]

        def enter(n, rows):
            acts[n % 2][rows, :] = dot_nn(x_ref[rows, :], in_ref[:, pieces[n]])
            hids[n % 2][rows, :] = dot_nt(grad_res[rows, :], out_ref[pieces[n], :])

        def activate(n, rows):
            for at in range(rows.start, rows.stop, 32):
                some = slice(at, at + 32)
                act, grad_hidden = acts[n % 2][some, :], hids[n % 2][some, :]
                bell = jnp.exp2(act * act * (-0.5 * LOG2_E))
                base = 1.0 + (ERFC_P * 2.0**-0.5) * jnp.abs(act)
                t = pl.reciprocal(base, approx=True)
                t = t * (2.0 - base * t)
                poly = 0.5 * ERFC_C[-1]
                for coefficient in ERFC_C[-2::-1]:
                    poly = poly * t + 0.5 * coefficient
                tail = poly * (t * bell)
                share = jnp.where(act >= 0.0, 1.0 - tail, tail)
                hidden_ref[some, pieces[n]] = (act * share).astype(BF)
                slope = share + act * (bell * 0.3989422804014327)
                inner_ref[some, pieces[n]] = (grad_hidden * slope).astype(BF)

        def leave(first, last, rows):
            part = slice(first * tile, last * tile)
            res_sum[rows, :] += dot_nn(hidden_ref[rows, part], out_ref[part, :])
            back_sum[rows, :] += dot_nt(inner_ref[rows, part], in_ref[:, part])

        for rows in spans:
            enter(0, rows)
        for n in range(count):
            for rows in spans:
                if n + 1 < count:
                    enter(n + 1, rows)
                elif n:
                    leave(0, n, rows)
                activate(n, rows)
        for rows in spans:
            leave(count - 1, count, rows)

    work()
    if not far:
        return

    @pl.when(step == steps - 1)
    def _():
        for e in range(experts):
            rows = slice(e * half, (e + 1) * half)
            res = res_sum[rows, :].astype(BF)
            res_ref[e] = res
            gate = jnp.sum(dy_ref[e].astype(F32) * res.astype(F32), axis=1, keepdims=True)
            line = jnp.sum(jnp.where(diag, gate, 0.0), axis=0, keepdims=True)
            pieces = [p.astype(F32) for p in split_three(line)]
            line = jnp.concatenate(pieces + [jnp.zeros((1, width - 3 * LANES), F32)], axis=1)
            back = jnp.where(iota((half, width), 0) == 0, line, back_sum[rows, :])
            back_ref[e] = back.astype(BF)


def hidden_block(hidden):
    return next(b for b in (768, 512, 384, 256, 128) if hidden % b == 0)


def call_experts(sz, c, ring, x, dy, own, far, before=(), res=None):
    width, half, chunk, experts = sz.width, sz.half, sz.chunk, sz.experts
    hidden = (own[0] if own else far[0][0]).shape[-1]
    block = hidden_block(hidden)
    per_ring = hidden // block
    steps = per_ring * ((1 if own else 0) + (ring - 1 if far else 0))
    last = bool(far) or ring == 1
    rows_spec = pl.BlockSpec((experts, half, width), lambda s: (0, 0, 0))
    flat_spec = pl.BlockSpec((chunk, width), lambda s: (0, 0))
    wide_spec = pl.BlockSpec((chunk, block), lambda s: (0, s))
    any_spec = pl.BlockSpec(memory_space=pl.ANY)
    weights = [*own, *(far[0] if far else []), *(far[1] if far else [])]
    tile = 256 if block % 256 == 0 else 128
    flat = lambda kind: jax.ShapeDtypeStruct((chunk, width), kind)
    rows = jax.ShapeDtypeStruct((experts, half, width), BF)
    both = jax.ShapeDtypeStruct((experts, 2 * half, width), BF)
    chunk_spec = pl.BlockSpec((experts, half, width), lambda s: (0, c, 0))
    wide = jax.ShapeDtypeStruct((chunk, steps * block), BF)
    out_specs, out_shape = [wide_spec, wide_spec], [wide, wide]
    if own:
        out_specs, out_shape = out_specs + [flat_spec], out_shape + [flat(BF)]
    sums = [pltpu.VMEM((chunk, width), F32)] * 2
    if last:
        out_specs, out_shape = out_specs + [chunk_spec, rows_spec], out_shape + [both, rows]
    else:
        out_specs, out_shape, sums = out_specs + [flat_spec] * 2, out_shape + [flat(F32)] * 2, []
    counts = (len(far[0]), len(far[1])) if far else (0, 0)
    given = [] if res is None else [res]
    return pl.pallas_call(
        functools.partial(
            expert_kernel, sz, ring, per_ring, bool(own), last, len(given), *counts
        ),
        grid=(steps,),
        in_specs=[flat_spec, pl.BlockSpec((experts, half, width), lambda s: (0, c, 0))]
        + [any_spec] * len(weights)
        + [flat_spec] * len(before)
        + [any_spec] * len(given),
        input_output_aliases={2 + len(weights) + len(before): 3} if given else {},
        out_specs=out_specs,
        out_shape=out_shape,
        scratch_shapes=sums
        + [pltpu.VMEM((chunk, tile), F32)] * 4
        + [
            pltpu.VMEM((steps, width, block), BF),
            pltpu.VMEM((steps, block, width), BF),
            pltpu.SemaphoreType.DMA((steps * (2 + sum(counts)),)),
        ],
        compiler_params=kernel_params(56),
        cost_estimate=SMALL_COST,
        name="experts",
    )(x, dy, *weights, *before, *given)


def weight_grad_kernel(
    x_one, x_two, grad_one, grad_two, hid_one, hid_two, inn_one, inn_two, _early, *refs
):
    x_t, grad_t = refs[-2:]
    count = (len(refs) - 2) // 2
    gi_refs, go_refs = refs[:count], refs[count : 2 * count]
    chunk = x_one.shape[0]

    @pl.when(pl.program_id(0) == 0)
    def _():
        x_t[:, :chunk] = x_one[...].T
        x_t[:, chunk:] = x_two[...].T
        grad_t[:, :chunk] = grad_one[...].T
        grad_t[:, chunk:] = grad_two[...].T

    grad_in = dot_nn(x_t[:, :chunk], inn_one[...]) + dot_nn(x_t[:, chunk:], inn_two[...])
    at = 0
    for ref in gi_refs:
        ref[...] = grad_in[at : at + ref.shape[0]].astype(ref.dtype)
        at += ref.shape[0]
    grad_out = dot_nn(grad_t[:, :chunk], hid_one[...]) + dot_nn(grad_t[:, chunk:], hid_two[...])
    grad_out = grad_out.T
    at = 0
    for ref in go_refs:
        ref[...] = grad_out[:, at : at + ref.shape[1]].astype(ref.dtype)
        at += ref.shape[1]


def call_weight_grads(sz, ring, hidden, far, flats, wides, early):
    width, chunk = sz.width, sz.chunk
    block = next(b for b in (512, 384, 256, 128) if hidden % b == 0)
    per_ring = hidden // block
    count = (ring - 1) * per_ring if far else per_ring
    flat_spec = pl.BlockSpec((chunk, width), lambda s: (0, 0))
    wide_spec = lambda first: pl.BlockSpec((chunk, block), lambda s: (0, first + s))
    wide_specs = [wide_spec(per_ring if far and whole else 0) for _array, whole in wides]
    if far:
        in_cuts, out_cuts = (width * 3 // 8, width * 5 // 8), (width // 3, width - width // 3)
        out_specs = [
            pl.BlockSpec((None, part, block), lambda s: (s // per_ring, 0, s % per_ring))
            for part in in_cuts
        ] + [
            pl.BlockSpec((None, block, part), lambda s: (s // per_ring, s % per_ring, 0))
            for part in out_cuts
        ]
        out_shape = [jax.ShapeDtypeStruct((ring - 1, part, hidden), BF) for part in in_cuts] + [
            jax.ShapeDtypeStruct((ring - 1, hidden, part), BF) for part in out_cuts
        ]
    else:
        out_specs = (
            pl.BlockSpec((width, block), lambda s: (0, s)),
            pl.BlockSpec((block, width), lambda s: (s, 0)),
        )
        out_shape = (
            jax.ShapeDtypeStruct((width, hidden), BF),
            jax.ShapeDtypeStruct((hidden, width), BF),
        )
    return pl.pallas_call(
        weight_grad_kernel,
        grid=(count,),
        in_specs=[flat_spec] * 4 + wide_specs + [pl.BlockSpec(memory_space=pl.ANY)],
        out_specs=out_specs,
        out_shape=out_shape,
        scratch_shapes=[pltpu.VMEM((width, 2 * chunk), BF), pltpu.VMEM((width, 2 * chunk), BF)],
        compiler_params=kernel_params(56),
        cost_estimate=pl.CostEstimate(
            flops=8 * chunk * width * block * count,
            bytes_accessed=8 * chunk * block * count + 8 * width * block * count,
            transcendentals=0,
        ),
        name="weight_grads",
    )(*flats, *(array for array, _whole in wides), early)


def combine_kernel(
    sz,
    back_one_ref,
    back_two_ref,
    slot_ref,
    slot_col_ref,
    gate_ref,
    routes_ref,
    proj_ref,
    tail_ref,
    dy_ref,
    after_ref,
    normed_ref,
    mixed_ref,
    _early,
    grad_after_ref,
    grad_mixed_ref,
    proj_grad_ref,
    small_ref,
    tail_t,
    from_router,
    branch_all,
):
    width, seq, rows, half, chunk = sz.width, sz.seq_pad, sz.rows, sz.half, sz.chunk
    step = pl.program_id(0)
    first = sz.experts

    @pl.when(step == 0)
    def _():
        tail_t[...] = tail_ref[...].astype(F32).T
        group = max(1, LANES // half)
        metas = []
        for ref in (back_one_ref, back_two_ref):
            for e0 in range(0, sz.experts, group):
                line = jnp.zeros((1, 3 * LANES), F32)
                for g in range(group):
                    at = (e0 + g) * half
                    one = ref[at : at + 16, 0 : 3 * LANES].astype(F32)
                    pieces = [one[:, m * LANES : (m + 1) * LANES] for m in range(3)]
                    if g:
                        pieces = [pltpu.roll(p, g * half, axis=1) for p in pieces]
                    line += jnp.concatenate([p[0:1] for p in pieces], axis=1)
                metas.append(line)
        part = iota((16, 2 * chunk), 0)
        coded = jnp.zeros((16, 2 * chunk), F32)
        for m in range(3):
            line = jnp.concatenate([x[:, m * LANES : (m + 1) * LANES] for x in metas], axis=1)
            coded = jnp.where(part == m, line, coded)
        coded = coded.astype(BF)
        grads = []
        for k in range(sz.choose):
            ids = iota((256, rows), 0)
            total = jnp.zeros((16, rows), F32)
            for start in range(0, 2 * chunk, 256):
                pick = ones_where(ids + start == slot_ref[k : k + 1]).astype(BF)
                total += dot_nn(coded[:, start : start + 256], pick)
            grads.append(jnp.sum(total, axis=0, keepdims=True))
        gates = [gate_ref[k : k + 1] for k in range(sz.choose)]
        mean_grad = functools.reduce(jnp.add, [g * v for g, v in zip(gates, grads)])
        kinds = iota((LANES, rows), 0)
        logits_grad = jnp.zeros((LANES, rows), F32)
        for k in range(sz.choose):
            chosen = gates[k] * (grads[k] - mean_grad)
            logits_grad = jnp.where(kinds == routes_ref[k : k + 1], chosen, logits_grad)
        logits_grad = logits_grad.astype(BF)
        small_ref[...] = dot_nn(logits_grad, normed_ref[...].reshape(rows, width))
        from_router[...] = dot_tn(logits_grad, tail_t[...].astype(BF))

    here = pl.ds(step * seq, seq)
    slot_col = slot_col_ref[here, :]
    upstream = from_router[here, :]
    for c, ref in enumerate((back_one_ref, back_two_ref)):
        ids = iota((seq, chunk), 1) + c * chunk
        pick = ids == slot_col[:, 0:1]
        for k in range(1, sz.choose):
            pick = pick | (ids == slot_col[:, k : k + 1])
        upstream += dot_nn(ones_where(pick).astype(BF), ref[...])
    normal, inv = norm_parts(after_ref[...])
    grad_after = dy_ref[...].astype(F32) + norm_back(
        upstream, tail_t[first + 2 : first + 3], normal, inv
    )
    live = iota((seq, 1), 0) < SEQ
    grad_after = jnp.where(live, grad_after, 0.0)
    upstream = jnp.where(live, upstream, 0.0)
    grad_after_ref[...] = grad_after
    branch = grad_after.astype(BF)
    branch_all[here, :] = branch
    grad_mixed_ref[...] = dot_nn(branch, proj_ref[...]).astype(BF)
    small_ref[first + 2 : first + 3, :] += jnp.sum(upstream * normal, axis=0, keepdims=True)
    small_ref[first + 3 : first + 4, :] += jnp.sum(upstream, axis=0, keepdims=True)

    @pl.when(step == sz.images - 1)
    def _():
        proj_grad_ref[...] = dot_tn(
            branch_all[...], mixed_ref[...].reshape(rows, width)
        ).astype(BF)


def call_combine(
    sz,
    back_one,
    back_two,
    slots,
    slot_col,
    gates,
    routes_row,
    packed,
    dy,
    attended,
    normed,
    mixed,
    early,
):
    images, seq, width, rows = sz.images, sz.seq_pad, sz.width, sz.rows
    per_image = lambda size: pl.BlockSpec((None, seq, size), lambda i: (i, 0, 0))
    whole = lambda *shape: pl.BlockSpec(shape, lambda i: (0,) * len(shape))
    return pl.pallas_call(
        functools.partial(combine_kernel, sz),
        grid=(images,),
        in_specs=[
            whole(sz.chunk, width),
            whole(sz.chunk, width),
            whole(8, rows),
            whole(rows, LANES),
            whole(8, rows),
            whole(8, rows),
            pl.BlockSpec((width, width), lambda i: (0, 1)),
            pl.BlockSpec((width, LANES), lambda i: (0, 2 * width // LANES)),
            per_image(width),
            per_image(width),
            whole(images, seq, width),
            whole(images, seq, width),
            pl.BlockSpec(memory_space=pl.ANY),
        ],
        out_specs=(
            per_image(width),
            per_image(width),
            whole(width, width),
            whole(LANES, width),
        ),
        out_shape=(
            jax.ShapeDtypeStruct((images, seq, width), F32),
            jax.ShapeDtypeStruct((images, seq, width), BF),
            jax.ShapeDtypeStruct((width, width), BF),
            jax.ShapeDtypeStruct((LANES, width), F32),
        ),
        scratch_shapes=[
            pltpu.VMEM((LANES, width), F32),
            pltpu.VMEM((rows, width), F32),
            pltpu.VMEM((rows, width), BF),
        ],
        compiler_params=kernel_params(56),
        cost_estimate=pl.CostEstimate(
            flops=4 * rows * width * width + 4 * rows * sz.chunk * width,
            bytes_accessed=rows * width * 16 + 4 * sz.chunk * width + 4 * width * width,
            transcendentals=0,
        ),
        name="combine",
    )(
        back_one,
        back_two,
        slots,
        slot_col,
        gates,
        routes_row,
        packed[1],
        packed[1],
        dy,
        attended,
        normed,
        mixed,
        early,
    )


def attend_back_kernel(
    sz,
    tok_ref,
    w_one_ref,
    w_two_ref,
    qkv_ref,
    lse_ref,
    grad_mixed_ref,
    grad_after_ref,
    proj_grad_ref,
    small_ref,
    core_ref,
    _early,
    tok_grad_ref,
    *refs,
):
    packed_refs = refs[:-4]
    tail_t, normed_all, grad_all, small_sum = refs[-4:]
    width, seq, rows = sz.width, sz.seq_pad, sz.rows
    step = pl.program_id(0)
    first = sz.experts

    @pl.when(step == 0)
    def _():
        tail_t[...] = w_two_ref[:, 2 * width :].astype(F32).T
        small_sum[...] = small_ref[...]

    here = pl.ds(step * seq, seq)
    gain, bias = tail_t[first : first + 1], tail_t[first + 1 : first + 2]
    normal, inv = norm_parts(tok_ref[...].astype(F32))
    normed_all[here, :] = (normal * gain + bias).astype(BF)
    key_ok = iota((seq, seq), 0) < SEQ
    pair_lane = iota((1, LANES), 1) // HEAD
    for j in range(HEADS // 2):
        at = j * LANES
        q = qkv_ref[:, at : at + LANES]
        key = qkv_ref[:, width + at : width + at + LANES]
        val = qkv_ref[:, 2 * width + at : 2 * width + at + LANES]
        grad = grad_mixed_ref[:, at : at + LANES]
        sum_q = jnp.zeros((seq, LANES), F32)
        sum_k = jnp.zeros((seq, LANES), F32)
        sum_v = jnp.zeros((seq, LANES), F32)
        for a in range(2):
            own = ones_where(pair_lane == a).astype(BF)
            scaled = own * HEAD**-0.5
            q_own, grad_own = q * scaled, grad * own
            scores = dot_nt(key, q_own)
            lse = lse_ref[2 * j + a : 2 * j + a + 1, :]
            probs = jnp.where(key_ok, jnp.exp(scores - lse), 0.0)
            grad_probs = dot_nt(val, grad_own)
            sum_v += dot_nn(probs.astype(BF), grad_own)
            delta = jnp.sum(grad_probs * probs, axis=0, keepdims=True)
            grad_scores = (probs * (grad_probs - delta)).astype(BF)
            sum_q += dot_tn(grad_scores, key * scaled)
            sum_k += dot_nn(grad_scores, q_own)
        grad_all[here, at : at + LANES] = sum_q.astype(BF)
        grad_all[here, width + at : width + at + LANES] = sum_k.astype(BF)
        grad_all[here, 2 * width + at : 2 * width + at + LANES] = sum_v.astype(BF)
    upstream = dot_nt(grad_all[here, : 2 * width], w_one_ref[...])
    upstream += dot_nt(grad_all[here, 2 * width :], w_two_ref[:, :width])
    tok_grad_ref[...] = grad_after_ref[...] + norm_back(upstream, gain, normal, inv)
    small_sum[first : first + 1, :] += jnp.sum(upstream * normal, axis=0, keepdims=True)
    small_sum[first + 1 : first + 2, :] += jnp.sum(upstream, axis=0, keepdims=True)

    @pl.when(step == sz.images - 1)
    def _():
        parts = (
            dot_tn(normed_all[...], grad_all[...]),
            proj_grad_ref[...].astype(F32),
            small_sum[...].T,
        )
        if len(packed_refs) == 1:
            at = 0
            for part in parts:
                size = part.shape[1]
                packed_refs[0][:, at : at + size] = part.astype(BF)
                at += size
            return
        keep_one, send_one, keep_two, send_two = packed_refs
        n_dp, ring, shard, _ = keep_one.shape
        first_core = core_ref[0] == 0

        def put(keep, send, at, part, part_lanes):
            size = part_lanes.stop - part_lanes.start
            for d in range(n_dp):
                for r in range(ring):
                    row = (d * ring + r) * 2 * shard
                    zero = part[row : row + shard, part_lanes]
                    one = part[row + shard : row + 2 * shard, part_lanes]
                    place = (d, r) if keep is keep_one else (r, d)
                    keep[(*place, slice(None), slice(at, at + size))] = jnp.where(
                        first_core, zero, one
                    ).astype(BF)
                    send[(*place, slice(None), slice(at, at + size))] = jnp.where(
                        first_core, one, zero
                    ).astype(BF)

        put(keep_one, send_one, 0, parts[0], slice(0, 2 * width))
        put(keep_two, send_two, 0, parts[0], slice(2 * width, 3 * width))
        put(keep_two, send_two, width, parts[1], slice(0, width))
        put(keep_two, send_two, 2 * width, parts[2], slice(0, parts[2].shape[1]))


def call_attend_back(
    sz, tok, packed, qkv, lse, grad_mixed, grad_after, proj_grad, small, core, early, out_dims
):
    images, seq, width, rows = sz.images, sz.seq_pad, sz.width, sz.rows
    per_image = lambda size: pl.BlockSpec((None, seq, size), lambda i: (i, 0, 0))
    lse_spec = pl.BlockSpec((None, 16, seq), lambda i: (i, 0, 0))
    whole = lambda *shape: pl.BlockSpec(shape, lambda i: (0,) * len(shape))
    return pl.pallas_call(
        functools.partial(attend_back_kernel, sz),
        grid=(images,),
        in_specs=[
            per_image(width),
            whole(width, sz.part_one),
            whole(width, sz.part_two),
            per_image(3 * width),
            lse_spec,
            per_image(width),
            per_image(width),
            whole(width, width),
            whole(LANES, width),
            pl.BlockSpec(memory_space=pltpu.SMEM),
            pl.BlockSpec(memory_space=pl.ANY),
        ],
        out_specs=(per_image(width), *(whole(*dims) for dims in out_dims)),
        out_shape=(
            jax.ShapeDtypeStruct((images, seq, width), F32),
            *(jax.ShapeDtypeStruct(dims, BF) for dims in out_dims),
        ),
        scratch_shapes=[
            pltpu.VMEM((LANES, width), F32),
            pltpu.VMEM((rows, width), BF),
            pltpu.VMEM((rows, 3 * width), BF),
            pltpu.VMEM((LANES, width), F32),
        ],
        compiler_params=kernel_params(56),
        cost_estimate=pl.CostEstimate(
            flops=12 * rows * width * width + 10 * rows * seq * width,
            bytes_accessed=4 * width * sz.packed + rows * width * 18,
            transcendentals=rows * seq * HEADS,
        ),
        name="attend_back",
    )(tok, *packed, qkv, lse, grad_mixed, grad_after, proj_grad, small, core, early)


def output_kernel(sz, res_ref, slot_col_ref, gate_col_ref, after_ref, out_ref):
    seq, chunk = sz.seq_pad, sz.chunk
    here = pl.ds(pl.program_id(0) * seq, seq)
    slot_col = slot_col_ref[here, :]
    gate_col = gate_col_ref[here, :]
    moe = jnp.zeros((seq, sz.width), F32)
    for k in range(sz.choose):
        rows = jnp.zeros((seq, sz.width), F32)
        for c in range(2):
            ids = iota((seq, chunk), 1) + c * chunk
            res = res_ref[:, c * sz.half : (c + 1) * sz.half, :].reshape(chunk, sz.width)
            rows += dot_nn(ones_where(ids == slot_col[:, k : k + 1]).astype(BF), res)
        moe += gate_col[:, k : k + 1] * rows
    out_ref[...] = (after_ref[...] + moe).astype(BF)


def call_output(sz, res, slot_col, gate_col, after):
    images, seq, width, rows = sz.images, sz.seq_pad, sz.width, sz.rows
    per_image = pl.BlockSpec((None, seq, width), lambda i: (i, 0, 0))
    whole = lambda *shape: pl.BlockSpec(shape, lambda i: (0,) * len(shape))
    return pl.pallas_call(
        functools.partial(output_kernel, sz),
        grid=(images,),
        in_specs=[
            whole(sz.experts, 2 * sz.half, width),
            whole(rows, LANES),
            whole(rows, LANES),
            per_image,
        ],
        out_specs=per_image,
        out_shape=jax.ShapeDtypeStruct((images, seq, width), BF),
        compiler_params=kernel_params(24),
        cost_estimate=SMALL_COST,
        name="output",
    )(res, slot_col, gate_col, after)


def adam_update(weight, gradient, moment_one, moment_two, clip_scale, rate_val, decay_val):
    clipped = gradient * clip_scale
    first_new = BETA_ONE * moment_one + (1.0 - BETA_ONE) * clipped
    second_new = BETA_TWO * moment_two + (1.0 - BETA_TWO) * clipped * clipped
    first_hat = first_new / (1.0 - BETA_ONE**STEP)
    second_hat = second_new / (1.0 - BETA_TWO**STEP)
    return (
        first_new,
        second_new,
        weight - rate_val * (first_hat / (jnp.sqrt(second_hat) + ADAM_EPS) + decay_val * weight),
    )


def exchange(array):
    return lax.all_to_all(array, GROUP, split_axis=0, concat_axis=0, tiled=True)


class Gather:
    def __init__(self, array):
        self.rank, self.done, self.array = {}, [], array
        for axis in ALL:
            for bit in reversed(range(lax.axis_size(axis).bit_length() - 1)):
                self.rank[axis, bit] = len(self.rank)

    def bits(self, axis):
        return [key for key in self.rank if key[0] == axis]

    def advance(self, keys):
        for key in keys:
            self.double(*key)
        return self.array

    def part(self, lanes):
        other = Gather(self.array[..., lanes])
        other.done = list(self.done)
        return other

    def double(self, axis, bit):
        array, flip = self.array, 1 << bit
        other = lax.ppermute(array, axis, [(s, s ^ flip) for s in range(lax.axis_size(axis))])
        at = sum(self.rank[key] < self.rank[axis, bit] for key in self.done)
        here = (lax.axis_index(axis) >> bit) & 1
        side = lax.broadcasted_iota(jnp.int32, (1,) * at + (2,) + (1,) * (array.ndim - at), at)
        self.array = jnp.where(side == here, jnp.expand_dims(array, at), jnp.expand_dims(other, at))
        self.done.append((axis, bit))

    def wait(self, *others):
        self.array = after(self.array, *others)


def scatter_ring(grads, axis):
    count, here = lax.axis_size(axis), lax.axis_index(axis)
    pick = lambda at: lax.dynamic_index_in_dim(grads, at % count, 0, keepdims=False)
    total = pick(here).astype(F32)
    for r in range(1, count):
        ahead = [(s, (s + r) % count) for s in range(count)]
        total += lax.ppermute(pick(here + r), axis, ahead).astype(F32)
    return total


def after(array, *others):
    return lax.optimization_barrier((array, *others))[0]


def on_device(
    tokens,
    out_grad,
    routes,
    slot_order,
    norm_params,
    qkv_weight,
    proj_weight,
    router_weight,
    inner_weight,
    outer_weight,
    norm_moment,
    norm_second,
    qkv_moment,
    qkv_second,
    proj_moment,
    proj_second,
    router_moment,
    router_second,
    inner_moment,
    inner_second,
    outer_moment,
    outer_second,
):
    tok_count, width = tokens.shape
    choose = routes.shape[1]
    experts = router_weight.shape[1]
    sz = Sizes(tok_count, width, choose, experts)
    images, seq, rows = sz.images, sz.seq_pad, sz.rows
    ring = lax.axis_size("row")
    n_dp, n_col = lax.axis_size("dp"), lax.axis_size("col")
    shard = qkv_weight.shape[0]

    gather = Gather(
        jnp.concatenate(
            [
                qkv_weight.astype(BF).reshape(shard, 3 * width),
                proj_weight.astype(BF),
                router_weight.astype(BF),
                norm_params.astype(BF),
                jnp.zeros((shard, sz.packed - 4 * width - experts - 4), BF),
            ],
            axis=1,
        )
    )
    in_own = lax.optimization_barrier(inner_weight[0].astype(BF))
    out_own = lax.optimization_barrier(outer_weight[0].astype(BF))

    def from_ahead(array, r):
        return lax.ppermute(array, "row", [(s, (s - r) % ring) for s in range(ring)])

    def to_ahead(array, r):
        return lax.ppermute(array, "row", [(s, (s + r) % ring) for s in range(ring)])

    def from_row(array):
        if ring == 1:
            return array[None]
        return jnp.stack([from_ahead(array, r) for r in range(1, ring)])

    cut = width // 4
    in_top = [from_row(in_own[:cut]), from_row(in_own[cut : 2 * cut])]

    def pad_rows(array):
        array = array.reshape(images, SEQ, array.shape[1])
        return jnp.pad(array, ((0, 0), (0, seq - SEQ), (0, 0)))

    tok_pad, dy_pad = pad_rows(tokens), pad_rows(out_grad)
    order = slot_order[0]
    order = (order % choose) * rows + order // choose
    order = jnp.pad(order, (0, sz.rank - sz.pairs), constant_values=-1).reshape(1, sz.rank)
    fill = ((0, 0), (0, rows - tok_count))
    routes_flat = jnp.pad(routes.T, fill, constant_values=-1).reshape(1, choose * rows)
    dy_flat = jnp.pad(out_grad, ((0, rows - tok_count), (0, 0)))
    flat_slots, dy_send = call_slots(sz, order, routes_flat, dy_flat)
    slots = jnp.pad(
        flat_slots[:, :tok_count].reshape(8, images, SEQ),
        ((0, 0), (0, 0), (0, seq - SEQ)),
        constant_values=-1,
    ).reshape(8, rows)
    slot_col = jnp.pad(slots.T, ((0, 0), (0, LANES - 8)))
    routes_row = jnp.pad(
        slots[choose : 2 * choose], ((0, 8 - choose), (0, 0)), constant_values=-1
    )
    dp_bits, row_bits, col_bits = gather.bits("dp"), gather.bits("row"), gather.bits("col")
    gather.advance(dp_bits[:-1])
    gather.wait(flat_slots, in_top[0])
    part_one = gather.part(slice(0, sz.part_one))
    part_two = gather.part(slice(sz.part_one, sz.packed))
    part_one.advance(dp_bits[-1:])
    part_two.advance(dp_bits[-1:])
    dy_there = exchange(after(dy_send, part_one.array, part_two.array, in_top[1]))
    one_row = part_one.advance(row_bits)
    part_one.wait(tok_pad, out_own)
    part_one = part_one.advance(col_bits)
    part_two = part_two.advance(row_bits + col_bits)
    packed = (part_one.reshape(width, sz.part_one), part_two.reshape(width, sz.part_two))
    in_far = [*in_top, from_row(after(in_own[2 * cut :], one_row))]
    cut = out_own.shape[0] * 9 // 32 // 16 * 16
    out_far = [from_row(after(out_own[:cut], one_row)), from_row(out_own[cut:])]

    qkv, lse, mixed, attended, normed, gates, gate_col, send_one, send_two = call_attend(
        sz, tok_pad, packed, routes_row, slots
    )

    def exchange_rows(array):
        return exchange(array.reshape(experts, sz.half, width)).reshape(sz.chunk, width)

    x_one = exchange_rows(after(send_one, dy_there, in_far[2], out_far[0]))
    x_two = exchange_rows(after(send_two, x_one, out_far[1], dy_pad, slot_col))
    own, far = [in_own, out_own], [in_far, out_far] if ring > 1 else None
    hidden_one, inner_one, grad_one, res_one, back_one = call_experts(
        sz, 0, ring, x_one, dy_there, own, far
    )
    hidden_two, inner_two, grad_two, res_both, back_two = call_experts(
        sz, 1, ring, x_two, dy_there, own, far, res=res_one
    )
    wides = [(array, True) for array in (hidden_one, hidden_two, inner_one, inner_two)]
    flats = (x_one, x_two, grad_one, grad_two)
    first_back = back_two
    back_one = exchange(back_one).reshape(sz.chunk, width)
    back_two = exchange(back_two).reshape(sz.chunk, width)
    hidden = in_own.shape[1]
    away = None
    if ring > 1:
        away = call_weight_grads(sz, ring, hidden, True, flats, wides, first_back)
    in_grad, out_grad_own = call_weight_grads(
        sz, ring, hidden, False, flats, wides, first_back if away is None else away[0]
    )
    kept_grads = (in_grad, out_grad_own)
    in_sent, out_sent = [[], []], [[], []]
    if ring > 1:
        send = lambda array: [to_ahead(part, r + 1) for r, part in enumerate(array)]
        in_sent, out_sent = [send(away[0]), send(away[1])], [send(away[2]), send(away[3])]
        for top, low in zip(*in_sent):
            in_grad = in_grad.astype(F32) + jnp.concatenate([top, low]).astype(F32)
        for top, low in zip(*out_sent):
            out_grad_own = out_grad_own.astype(F32) + jnp.concatenate([top, low], axis=1).astype(F32)
    res = exchange(after(res_both, *kept_grads, *in_sent[0]))

    grad_after, grad_mixed, proj_grad, small = call_combine(
        sz,
        back_one,
        back_two,
        slots,
        slot_col,
        gates,
        routes_row,
        packed,
        dy_pad,
        attended,
        normed,
        mixed,
        kept_grads[0],
    )
    direct = shard % 8 == 0 and n_col == 2
    one_dims = (n_dp, ring, shard, sz.part_one)
    two_dims = (ring, n_dp, shard, sz.part_two)
    core = lax.axis_index("col")
    tok_grad, *packed_grads = call_attend_back(
        sz,
        tok_pad,
        packed,
        qkv,
        lse,
        grad_mixed,
        grad_after,
        proj_grad,
        small,
        core.astype(jnp.int32).reshape(1),
        kept_grads[0],
        [one_dims, one_dims, two_dims, two_dims] if direct else [(width, sz.packed)],
    )
    block_out = call_output(sz, res, slot_col, gate_col, attended)

    if direct:
        keep_one, send_one, keep_two, send_two = packed_grads
        swap = lambda sent: lax.ppermute(sent, "col", [(0, 1), (1, 0)]).astype(F32)
        sum_one = keep_one.astype(F32) + swap(after(send_one, *in_sent[1], *out_sent[0]))
        sum_two = keep_two.astype(F32) + swap(after(send_two, *in_sent[1], *out_sent[0]))
    else:
        grads = packed_grads[0].reshape(n_dp, ring, n_col, shard, sz.packed)
        grads = scatter_ring(grads.transpose(2, 0, 1, 3, 4), "col")
        sum_one = grads[..., : sz.part_one]
        sum_two = grads[..., sz.part_one :].transpose(1, 0, 2, 3)

    def scatter_dp(grads):
        return lax.all_to_all(grads.astype(BF), "dp", split_axis=0, concat_axis=0, tiled=True)

    sum_one = jnp.sum(scatter_dp(after(sum_one, res)).astype(F32), axis=0)
    sum_two = scatter_ring(after(sum_two.astype(BF), *out_sent[1], block_out), "row")
    block_out = block_out[:, :SEQ].reshape(tok_count, width)
    tok_grad = tok_grad[:, :SEQ].reshape(tok_count, width)
    parts = scatter_dp(after(sum_two, sum_one, block_out, tok_grad))
    share_one = scatter_ring(sum_one.astype(BF), "row")
    share_two = jnp.sum(parts.astype(F32), axis=0)
    share = jnp.concatenate([share_one, share_two], axis=1)
    qkv_share = share[:, : 3 * width].reshape(shard, 3, width)
    proj_share = share[:, 3 * width : 4 * width]
    router_share = share[:, 4 * width : 4 * width + experts]
    norm_share = share[:, 4 * width + experts : 4 * width + experts + 4]

    in_grad, out_grad_own = in_grad.astype(F32), out_grad_own.astype(F32)
    local_square = (
        jnp.sum(share * share) + jnp.sum(in_grad * in_grad) + jnp.sum(out_grad_own * out_grad_own)
    )
    count = n_dp * ring * n_col
    squares = lax.all_to_all(
        jnp.broadcast_to(local_square, (count, 1, LANES)), ALL, split_axis=0, concat_axis=0, tiled=True
    )
    square_sum = jnp.sum(squares[:, 0, 0])
    grad_norm = jnp.sqrt(square_sum)
    clip_scale = jnp.minimum(1.0, CLIP_NORM / (grad_norm + 1e-06))
    outs = [
        block_out,
        tok_grad,
        grad_norm,
    ]
    outs += adam_update(
        norm_params, norm_share, norm_moment, norm_second, clip_scale, RATE_NORM, 0.0
    )
    for weight, grad, moment, second in (
        (qkv_weight, qkv_share, qkv_moment, qkv_second),
        (proj_weight, proj_share, proj_moment, proj_second),
        (router_weight, router_share, router_moment, router_second),
        (inner_weight, in_grad[None], inner_moment, inner_second),
        (outer_weight, out_grad_own[None], outer_moment, outer_second),
    ):
        outs += adam_update(weight, grad, moment, second, clip_scale, RATE_MATRIX, DECAY_MATRIX)
    return tuple(outs)


def solution(mesh):
    rows = P(ALL, None)
    cube = P(ALL, None, None)
    inner = P(GROUP, None, "row")
    outer = P(GROUP, "row", None)
    return jax.shard_map(
        on_device,
        mesh=mesh,
        in_specs=(rows,) * 5
        + (cube, rows, rows, inner, outer)
        + (rows, rows, cube, cube, rows, rows, rows, rows, inner, inner, outer, outer),
        out_specs=(rows, rows, P())
        + (rows,) * 3
        + (cube,) * 3
        + (rows,) * 6
        + (inner,) * 3
        + (outer,) * 3,
        check_vma=False,
    )
```

time: 1060 us -> 494 us (0.47)
  matrix products: 316 us -> 0 us
  blocking collectives: 218 us -> 0 us
  Pallas kernels: 0 us -> 191 us
  local copies, waits for them, and re-layouts: 208 us -> 42.5 us
  starting transfers between devices: 30.4 us -> 86.2 us
  waiting for transfers between devices: 149 us -> 94.2 us
  other arithmetic: 105 us -> 66.2 us
  between operations: 21.5 us -> 5.39 us
    dot_general x21 -> x0, matrix products: 316 us -> none  [the longest x1 69.1 us: on_device(): jnp.einsum('sjcd,jfd->sjcf', grad_arrived, outer_full, preferred_element_...]
    pallas_call x0 -> x9, Pallas kernels: none -> 191 us  [the longest x2 68.7 us: call_experts(): pl.pallas_call(functools.partial(expert_kernel, sz, ring, per_ring, bool(...]
    all_gather x2 -> x0, blocking collectives: 126 us -> none  [the longest x1 83.2 us: on_device(): lax.all_gather(router_weight.astype(low_type), ('dp', 'row', 'col'), axis...]
    reduce_scatter x4 -> x0, waiting for transfers between devices: 124 us -> none  [the longest x1 122 us: on_device(): lax.psum_scatter(qkv_grad, ('dp', 'row', 'col'), scatter_dimension=0, til...]
    ppermute x0 -> x21, waiting for transfers between devices: none -> 81.5 us  [the longest x5 35 us: from_ahead(): lax.ppermute(array, 'row', [(s, (s - r) % ring) for s in range(ring)])]
    gather x10 -> x0, local copies, waits for them, and re-layouts: 61 us -> none  [the longest x5 21 us: on_device(): jnp.take_along_axis(logits, routes, axis=1)]
    unnamed x1 -> x0, blocking collectives: 51.7 us -> none
    psum x1 -> x0, blocking collectives: 40 us -> none  [on_device(): square_sum = lax.psum(local_square, ('dp', 'row', 'col'))]
  transfers between devices with their start and end apart: 12 -> 30, of which waited for: 3 -> 15; matrix products, arithmetic and copies ran while one was open for 52% -> 14% of each run, Pallas kernels for 0% -> 39%
where the time goes in v1:
time: 494 us; the launch traced here: 486 us
  Pallas kernels  191 us (39%)
  waiting for transfers between devices  94.2 us (19%)
  starting transfers between devices  86.2 us (17%)
  other arithmetic  66.2 us (13%)
  local copies, waits for them, and re-layouts  42.5 us (9%)
  between operations  5.39 us (1%)
    pallas_call x2, Pallas kernels, call_experts(): pl.pallas_call(functools.partial(expert_kernel, sz, ring, per_ring, bool(...  68.7 us
    all_to_all x6, starting transfers between devices, exchange(): return lax.all_to_all(array, GROUP, split_axis=0, concat_axis=0, tiled=True)  36.6 us
    pallas_call x2, Pallas kernels, call_weight_grads(): pl.pallas_call(weight_grad_kernel, grid=(count,), in_specs=[flat_spec] *...  35.4 us
    ppermute x5, waiting for transfers between devices, from_ahead(): lax.ppermute(array, 'row', [(s, (s - r) % ring) for s in range(ring)])  35 us
    pallas_call x1, Pallas kernels, call_attend_back(): pl.pallas_call(functools.partial(attend_back_kernel, sz), grid=(images,),...  28.8 us
    ppermute x8, waiting for transfers between devices, double(): lax.ppermute(array, axis, [(s, s ^ flip) for s in range(lax.axis_size(axi...  28 us
    sub x6, other arithmetic, adam_update(): weight - rate_val * (first_hat / (jnp.sqrt(second_hat) + ADAM_EPS) + deca...  26.1 us
    pallas_call x1, Pallas kernels, call_attend(): pl.pallas_call(functools.partial(attend_kernel, sz), grid=(images,), in_s...  24 us
  transfers between devices with their start and end apart: 30, of which 15 were waited for; matrix products, arithmetic and copies ran while one was open for 14% of the time, Pallas kernels for 39%

profile of v1, /device:TPU:0, one launch (start us, length us, event | category | flops | bytes accessed | tf_op | source)
XLA Modules:
  0.0 485.6 jit_solution(15202585913465529626)
XLA Ops:
  4.2 4.1 collective-permute-start
  8.3 2.6 convert_bitcast_fusion.1.refs_2_
  19.0 10.5 %slots.1 = (s32[8,896]{1,0:T(8,128)}, bf16[16,128,768]{2,1,0:T(8,128)(2,1)}) custom-call(s32[1,1792]{1,0:T(1,128)} %reshape.159.order_ref, s32[1,1792]{1,0:T(1,128)} %bitcast.96, bf16[896,768]{1,0:T(8,128)(2,1)} %pad.34.dy_ref), custom_call_target="tpu_custom_call" | custom-call | flops 1024 | bytes 1024 | tf_op jit(solution)/shard_map/slots/pallas_call | solution.py:176
  33.5 6.4 %collective-permute-done.3 = bf16[2,2,24,1536]{3,2,1,0:T(8,128)(2,1)S(1)} collective-permute-done((bf16[2,2,24,1536]{3,2,1,0:T(8,128)(2,1)S(1)}, bf16[2,2,24,1536]{3,2,1,0:T(8,128)(2,1)S(1)}, u32[]{:S(2)}, u32[]{:S(2)}) %collective-permute-start.3) | collective-permute-done | bytes 294944 | tf_op jit(solution)/shard_map/ppermute | solution.py:1031
  40.8 4.6 collective-permute-done.6
  47.1 5.3 %all-to-all-start = ((bf16[16,128,768]{2,1,0:T(8,128)(2,1)}), bf16[16,128,768]{2,1,0:T(8,128)(2,1)}, u32[]{:S(2)}, u32[]{:S(2)}) async-start(bf16[16,128,768]{2,1,0:T(8,128)(2,1)} %get-tuple-element.76), calls=%async_computation | async-start | bytes 6291456 | tf_op jit(solution)/shard_map/all_to_all | solution.py:1006
  53.9 2.6 convert_bitcast_fusion.refs_3_
  56.5 3.5 reshape.157
  60.0 2.5 pad.31.tok_ref
  63.1 6.7 %collective-permute-done.7 = bf16[2,2,2,24,1664]{4,3,2,1,0:T(8,128)(2,1)} collective-permute-done((bf16[2,2,2,24,1664]{4,3,2,1,0:T(8,128)(2,1)S(1)}, bf16[2,2,2,24,1664]{4,3,2,1,0:T(8,128)(2,1)}, u32[]{:S(2)}, u32[]{:S(2)}) %collective-permute-start.7) | collective-permute-done | bytes 639008 | tf_op jit(solution)/shard_map/ppermute | solution.py:1031
  69.7 2.5 broadcast_select_fusion
  72.2 9.7 %collective-permute-done.4 = bf16[2,2,2,24,1536]{4,3,2,1,0:T(8,128)(2,1)S(1)} collective-permute-done((bf16[2,2,2,24,1536]{4,3,2,1,0:T(8,128)(2,1)}, bf16[2,2,2,24,1536]{4,3,2,1,0:T(8,128)(2,1)S(1)}, u32[]{:S(2)}, u32[]{:S(2)}) %collective-permute-start.4) | collective-permute-done | bytes 589856 | tf_op jit(solution)/shard_map/ppermute | solution.py:1031
  96.0 3.3 bitcast_select_fusion.1.w_one_ref
  99.2 3.7 bitcast_select_fusion.w_two_ref.proj_ref.tail_ref
  103.0 24.0 %attend.1 = (bf16[4,224,2304]{2,1,0:T(8,128)(2,1)}, f32[4,16,224]{2,1,0:T(8,128)}, bf16[4,224,768]{2,1,0:T(8,128)(2,1)}, f32[4,224,768]{2,1,0:T(8,128)}, bf16[4,...) custom-call(bf16[4,224,768]{2,1,0:T(8,128)(2,1)} %pad.31.tok_ref, ...), custom_call_target="tpu_custom_call" | custom-call | flops 1024 | bytes 1024 | tf_op jit(solution)/shard_map/attend/pallas_call | solution.py:307
  127.1 5.8 %all-to-all-start.1 = ((bf16[16,64,768]{2,1,0:T(8,128)(2,1)}), bf16[16,64,768]{2,1,0:T(8,128)(2,1)}, u32[]{:S(2)}, u32[]{:S(2)}) async-start(bf16[16,64,768]{2,1,0:T(8,128)(2,1)} %bitcast.92), calls=%async_computation.1 | async-start | bytes 3145728 | tf_op jit(solution)/shard_map/all_to_all | solution.py:1006
  139.5 34.2 %collective-permute-done.12 = bf16[1104,768]{1,0:T(8,128)(2,1)S(1)} collective-permute-done((bf16[1104,768]{1,0:T(8,128)(2,1)}, bf16[1104,768]{1,0:T(8,128)(2,1)S(1)}, u32[]{:S(2)}, u32[]{:S(2)}) %collective-permute-start.12) | collective-permute-done | bytes 1695776 | tf_op jit(solution)/shard_map/ppermute | solution.py:1105
  173.7 5.8 %all-to-all-start.2 = ((bf16[16,64,768]{2,1,0:T(8,128)(2,1)}), bf16[16,64,768]{2,1,0:T(8,128)(2,1)S(1)}, u32[]{:S(2)}, u32[]{:S(2)}) async-start(bf16[16,64,768]{2,1,0:T(8,128)(2,1)} %bitcast.91), calls=%async_computation.2 | async-start | bytes 3145728 | tf_op jit(solution)/shard_map/all_to_all | solution.py:1006
  179.5 34.3 %experts.2 = (bf16[1024,3072]{1,0:T(8,128)(2,1)}, bf16[1024,3072]{1,0:T(8,128)(2,1)}, bf16[1024,768]{1,0:T(8,128)(2,1)}, bf16[16,128,768]{2,1,0:T(8,128)(2,1)}, bf16[16,64,768]{2,1,0:T(8,128)(2,1)}) custom-call(bf16[1024,768]{1,0:T(8,128)(2,1)} %bitcast.13.refs_0_.x_one, bf16[16,128,768]{2,1,0:T(8,128)(2,1)} %all-to-all-done.refs_1_, ...), custom_call_target="tpu_custom_call" | custom-call | flops 1024 | bytes 1024 | tf_op jit(solution)/shard_map/experts/pallas_call | solution.py:534
  213.8 7.1 %all-to-all-start.4 = ((bf16[16,64,768]{2,1,0:T(8,128)(2,1)}), bf16[16,64,768]{2,1,0:T(8,128)(2,1)S(1)}, u32[]{:S(2)}, u32[]{:S(2)}) async-start(bf16[16,64,768]{2,1,0:T(8,128)(2,1)} %get-tuple-element.98), calls=%async_computation.4 | async-start | bytes 3145728 | tf_op jit(solution)/shard_map/all_to_all | solution.py:1006
  221.0 34.3 %experts.3 = (bf16[1024,3072]{1,0:T(8,128)(2,1)}, bf16[1024,3072]{1,0:T(8,128)(2,1)}, bf16[1024,768]{1,0:T(8,128)(2,1)}, bf16[16,128,768]{2,1,0:T(8,128)(2,1)}, bf16[16,64,768]{2,1,0:T(8,128)(2,1)}) custom-call(bf16[1024,768]{1,0:T(8,128)(2,1)} %bitcast.78, bf16[16,128,768]{2,1,0:T(8,128)(2,1)} %all-to-all-done.refs_1_, ...), custom_call_target="tpu_custom_call", output_to_operand_aliasing={{3}: (9, {})} | custom-call | flops 1024 | bytes 1024 | tf_op jit(solution)/shard_map/experts/pallas_call | solution.py:534
  255.3 6.9 %all-to-all-start.5 = ((bf16[16,64,768]{2,1,0:T(8,128)(2,1)}), bf16[16,64,768]{2,1,0:T(8,128)(2,1)S(1)}, u32[]{:S(2)}, u32[]{:S(2)}) async-start(bf16[16,64,768]{2,1,0:T(8,128)(2,1)} %get-tuple-element.89._early), calls=%async_computation.5 | async-start | bytes 3145728 | tf_op jit(solution)/shard_map/all_to_all | solution.py:1006
  262.2 17.6 %weight_grads.2 = (bf16[1,288,1536]{2,1,0:T(8,128)(2,1)}, bf16[1,480,1536]{2,1,0:T(8,128)(2,1)}, bf16[1,1536,256]{2,1,0:T(8,128)(2,1)}, bf16[1,1536,512]{2,1,0:T(8,128)(2,1)}) custom-call(bf16[1024,768]{1,0:T(8,128)(2,1)} %bitcast.13.refs_0_.x_one, bf16[1024,768]{1,0:T(8,128)(2,1)} %bitcast.79, bf16[1024,768]{1,0:T(8,128)(2,1)} %get-tuple-element.83.grad_one, ...), custom_call_target="tpu_custom_call" | custom-call | flops 9663676416 | bytes 22020096 | tf_op jit(solution)/shard_map/weight_grads/pallas_call | solution.py:616
  281.4 17.7 %weight_grads.3 = (bf16[768,1536]{1,0:T(8,128)(2,1)}, bf16[1536,768]{1,0:T(8,128)(2,1)}) custom-call(bf16[1024,768]{1,0:T(8,128)(2,1)} %bitcast.13.refs_0_.x_one, bf16[1024,768]{1,0:T(8,128)(2,1)} %bitcast.80, bf16[1024,768]{1,0:T(8,128)(2,1)} %get-tuple-element.83.grad_one, bf16[1024,768]{1,0:T(8,128)(2,1)} %get-tuple-element.84.grad_two, ...), custom_call_target="tpu_custom_call" | custom-call | flops 9663676416 | bytes 22020096 | tf_op jit(solution)/shard_map/weight_grads/pallas_call | solution.py:616
  299.2 3.1 collective-permute-done.13
  303.5 5.8 %all-to-all-start.3 = ((bf16[16,128,768]{2,1,0:T(8,128)(2,1)}), bf16[16,128,768]{2,1,0:T(8,128)(2,1)S(1)}, u32[]{:S(2)}, u32[]{:S(2)}) async-start(bf16[16,128,768]{2,1,0:T(8,128)(2,1)} %get-tuple-element.93), calls=%async_computation.3 | async-start | bytes 6291456 | tf_op jit(solution)/shard_map/all_to_all | solution.py:1006
  311.3 17.1 %combine.1 = (f32[4,224,768]{2,1,0:T(8,128)}, bf16[4,224,768]{2,1,0:T(8,128)(2,1)}, bf16[768,768]{1,0:T(8,128)(2,1)}, f32[128,768]{1,0:T(8,128)}) custom-call(bf16[1024,768]{1,0:T(8,128)(2,1)} %bitcast.89, bf16[1024,768]{1,0:T(8,128)(2,1)} %bitcast.90, s32[8,896]{1,0:T(8,128)} %copy.196.slot_ref, s32[896,128]{1,0:T(8,128)} %pad.38.slot_col_ref, ...), custom_call_target="tpu_custom_call" | custom-call | flops 4932501504 | bytes 16515072 | tf_op jit(solution)/shard_map/combine/pallas_call | solution.py:749
  328.5 28.8 %attend_back.1 = (f32[4,224,768]{2,1,0:T(8,128)}, bf16[8,2,24,1536]{3,2,1,0:T(8,128)(2,1)}, bf16[8,2,24,1536]{3,2,1,0:T(8,128)(2,1)}, bf16[2,8,24,1664]{3,2,1,0:T(8,128)(2,1)}, bf16[2,8,24,1664]{3,2,1,0:T(8,128)(2,1)}) custom-call(bf16[4,224,768]{2,1,0:T(8,128)(2,1)} %pad.31.tok_ref, bf16[768,1536]{1,0:T(8,128)(2,1)} %bitcast_select_fusion.1.w_one_ref, ...), custom_call_target="tpu_custom_call" | custom-call | flops 7883194368 | bytes 22216704 | tf_op jit(solution)/shard_map/attend_back/pallas_call | solution.py:918
  357.3 3.6 collective-permute-done.15
  363.0 1.9 collective-permute-done.16
  364.9 2.6 convert_add_fusion.2
  368.6 15.3 %all-to-all-start.6 = ((bf16[8,2,24,1536]{3,2,1,0:T(8,128)(2,1)}), bf16[8,2,24,1536]{3,2,1,0:T(8,128)(2,1)}, u32[]{:S(2)}, u32[]{:S(2)}) async-start(bf16[8,2,24,1536]{3,2,1,0:T(8,128)(2,1)} %convert_add_fusion.2), calls=%async_computation.6 | async-start | bytes 2359296 | tf_op jit(solution)/shard_map/all_to_all | solution.py:1242
  384.0 2.1 add_convert_fusion
  386.7 6.6 %output.1 = bf16[4,224,768]{2,1,0:T(8,128)(2,1)S(1)} custom-call(bf16[16,128,768]{2,1,0:T(8,128)(2,1)S(1)} %all-to-all-done.3.res_ref, s32[896,128]{1,0:T(8,128)S(1)} %copy-done.2, f32[896,128]{1,0:T(8,128)S(1)} %copy-done.3, f32[4,224,768]{2,1,0:T(8,128)S(1)} %copy-done.1), custom_call_target="tpu_custom_call" | custom-call | flops 1024 | bytes 1024 | tf_op jit(solution)/shard_map/output/pallas_call | solution.py:975
  394.4 3.8 collective-permute-done.19
  399.8 3.3 slice.62
  403.1 3.5 reshape.172
  408.0 6.0 %collective-permute-done.20 = bf16[8,24,1664]{2,1,0:T(8,128)(2,1)} collective-permute-done((bf16[8,24,1664]{2,1,0:T(8,128)(2,1)S(1)}, bf16[8,24,1664]{2,1,0:T(8,128)(2,1)}, u32[]{:S(2)}, u32[]{:S(2)}) %collective-permute-start.20) | collective-permute-done | bytes 639008 | tf_op jit(solution)/shard_map/ppermute | solution.py:1048
  413.9 2.3 convert_add_fusion.3
  417.6 5.9 %all-to-all-start.7 = ((bf16[8,24,1664]{2,1,0:T(8,128)(2,1)}), bf16[8,24,1664]{2,1,0:T(8,128)(2,1)S(1)}, u32[]{:S(2)}, u32[]{:S(2)}) async-start(bf16[8,24,1664]{2,1,0:T(8,128)(2,1)} %convert_add_fusion.3), calls=%async_computation.7 | async-start | bytes 1277952 | tf_op jit(solution)/shard_map/all_to_all | solution.py:1242
  423.6 3.6 multiply_reduce_fusion.1
  428.8 3.2 multiply_reduce_fusion
  432.7 6.2 %all-to-all-done.7 = bf16[8,24,1664]{2,1,0:T(8,128)(2,1)S(1)} async-done(((bf16[8,24,1664]{2,1,0:T(8,128)(2,1)}), bf16[8,24,1664]{2,1,0:T(8,128)(2,1)S(1)}, u32[]{:S(2)}, u32[]{:S(2)}) %all-to-all-start.7) | async-done | bytes 639008 | tf_op jit(solution)/shard_map/all_to_all | solution.py:1242
  443.9 3.7 all-to-all-start.8
  449.2 5.4 %all-to-all-done.8 = f32[32,1,128]{2,1,0:T(1,128)S(1)} async-done(((f32[32,1,128]{2,1,0:T(1,128)}), f32[32,1,128]{2,1,0:T(1,128)S(1)}, u32[]{:S(2)}, u32[]{:S(2)}) %all-to-all-start.8) | async-done | bytes 16416 | tf_op jit(solution)/shard_map/all_to_all | solution.py:1262
  459.5 2.1 multiply_subtract_fusion.2
  462.9 11.4 %multiply_subtract_fusion = (f32[1,1536,768]{2,1,0:T(8,128)}, f32[1,1536,768]{2,1,0:T(8,128)}, f32[1,1536,768]{2,1,0:T(8,128)}) fusion(f32[1,1536,768]{2,1,0:T(8,128)} %param.31, f32[]{:T(128)S(6)} %min.3, bf16[1536,512]{1,0:T(8,128)(2,1)} %collective-permute-done.19, bf16[1536,256]{1,0:T(8,128)(2,1)} %copy-done.18, bf16[1536,768]{1,0:T(8,128)(2,1)S(1)} %copy-done.9, ...), kind=kLoop, calls=%fused_computation.8 | loop fusion | flops 25952256 | bytes 33030148 | tf_op jit(solution)/shard_map/sub | solution.py:1001
  475.0 9.0 %multiply_subtract_fusion.1 = (f32[1,768,1536]{2,1,0:T(8,128)}, f32[1,768,1536]{2,1,0:T(8,128)}, f32[1,768,1536]{2,1,0:T(8,128)}) fusion(f32[1,768,1536]{2,1,0:T(8,128)S(1)} %bitcast.75, f32[]{:T(128)S(6)} %min.3, bf16[480,1536]{1,0:T(8,128)(2,1)S(1)} %copy-done.13, bf16[288,1536]{1,0:T(8,128)(2,1)} %collective-permute-done.13, ...), kind=kLoop, calls=%fused_computation.9 | loop fusion | flops 25952256 | bytes 33030148 | tf_op jit(solution)/shard_map/sub | solution.py:1001
  (172 shorter events, 68.1 us)
Async XLA Ops:
  4.2 10.5 %copy-start.31 = (s32[1,1576]{1,0:T(1,128)S(1)}, s32[1,1576]{1,0:T(1,128)}, u32[]{:S(2)}) copy-start(s32[1,1576]{1,0:T(1,128)} %param.25) | copy-start | bytes 18916
  4.2 11.4 %collective-permute-start = (bf16[24,3200]{1,0:T(8,128)(2,1)S(1)}, bf16[24,3200]{1,0:T(8,128)(2,1)S(1)}, u32[]{:S(2)}, u32[]{:S(2)}) collective-permute-start(bf16[24,3200]{1,0:T(8,128)(2,1)S(1)} %concatenate.12), channel_id=1, source_target_pairs={{0,16},{4,20},{8,24},{12,28},{16,0},{20,4},{24,8},{28,12},{1,17},{... | collective-permute-start | bytes 460808 | tf_op jit(solution)/shard_map/ppermute | solution.py:1031
  13.2 16.6 %collective-permute-start.2 = (bf16[192,1536]{1,0:T(8,128)(2,1)S(1)}, bf16[192,1536]{1,0:T(8,128)(2,1)S(1)}, u32[]{:S(2)}, u32[]{:S(2)}) collective-permute-start(bf16[192,1536]{1,0:T(8,128)(2,1)S(1)} %get-tuple-element.264), channel_id=1, source_target_pairs={{0,2},{2,0},{1,3},{3,1},{4,6},{6,4},{5,7},{7,5},{8,10},{10,8},{9,1... | collective-permute-start | bytes 1769480 | tf_op jit(solution)/shard_map/ppermute | solution.py:1105
  15.7 13.8 %collective-permute-start.1 = (bf16[2,24,3200]{2,1,0:T(8,128)(2,1)S(1)}, bf16[2,24,3200]{2,1,0:T(8,128)(2,1)S(1)}, u32[]{:S(2)}, u32[]{:S(2)}) collective-permute-start(bf16[2,24,3200]{2,1,0:T(8,128)(2,1)S(1)} %broadcast_select_fusion.5), channel_id=1, source_target_pairs={{0,8},{4,12},{8,0},{12,4},{16,24},{20,28},{24,16},{28,20},{1,9},{5... | collective-permute-start | bytes 921608 | tf_op jit(solution)/shard_map/ppermute | solution.py:1031
  29.8 16.4 %copy-start.20 = (bf16[192,1536]{1,0:T(8,128)(2,1)}, bf16[192,1536]{1,0:T(8,128)(2,1)S(1)}, u32[]{:S(2)}) copy-start(bf16[192,1536]{1,0:T(8,128)(2,1)S(1)} %collective-permute-done.2) | copy-start | bytes 1769476
  29.9 10.0 %collective-permute-start.3 = (bf16[2,2,24,1536]{3,2,1,0:T(8,128)(2,1)S(1)}, bf16[2,2,24,1536]{3,2,1,0:T(8,128)(2,1)S(1)}, u32[]{:S(2)}, u32[]{:S(2)}) collective-permute-start(bf16[2,2,24,1536]{3,2,1,0:T(8,128)(2,1)S(1)} %slice.52), channel_id=1, source_target_pairs={{0,4},{4,0},{8,12},{12,8},{16,20},{20,16},{24,28},{28,24},{1,5},{5... | collective-permute-start | bytes 884744 | tf_op jit(solution)/shard_map/ppermute | solution.py:1031
  31.4 14.8 %collective-permute-start.9 = (bf16[192,1536]{1,0:T(8,128)(2,1)}, bf16[192,1536]{1,0:T(8,128)(2,1)S(1)}, u32[]{:S(2)}, u32[]{:S(2)}) collective-permute-start(bf16[192,1536]{1,0:T(8,128)(2,1)} %get-tuple-element.263), channel_id=1, source_target_pairs={{0,2},{2,0},{1,3},{3,1},{4,6},{6,4},{5,7},{7,5},{8,10},{10,8},{9,1... | collective-permute-start | bytes 1769480 | tf_op jit(solution)/shard_map/ppermute | solution.py:1105
  32.9 12.5 %collective-permute-start.6 = (bf16[2,2,24,1664]{3,2,1,0:T(8,128)(2,1)S(1)}, bf16[2,2,24,1664]{3,2,1,0:T(8,128)(2,1)S(1)}, u32[]{:S(2)}, u32[]{:S(2)}) collective-permute-start(bf16[2,2,24,1664]{3,2,1,0:T(8,128)(2,1)S(1)} %slice.53), channel_id=1, source_target_pairs={{0,4},{4,0},{8,12},{12,8},{16,20},{20,16},{24,28},{28,24},{1,5},{5... | collective-permute-start | bytes 958472 | tf_op jit(solution)/shard_map/ppermute | solution.py:1031
  47.1 80.0 %all-to-all-start = ((bf16[16,128,768]{2,1,0:T(8,128)(2,1)}), bf16[16,128,768]{2,1,0:T(8,128)(2,1)}, u32[]{:S(2)}, u32[]{:S(2)}) async-start(bf16[16,128,768]{2,1,0:T(8,128)(2,1)} %get-tuple-element.76), calls=%async_computation | async-start | bytes 6291456 | tf_op jit(solution)/shard_map/all_to_all | solution.py:1006
  52.4 17.3 %collective-permute-start.7 = (bf16[2,2,2,24,1664]{4,3,2,1,0:T(8,128)(2,1)S(1)}, bf16[2,2,2,24,1664]{4,3,2,1,0:T(8,128)(2,1)}, u32[]{:S(2)}, u32[]{:S(2)}) collective-permute-start(bf16[2,2,2,24,1664]{4,3,2,1,0:T(8,128)(2,1)S(1)} %broadcast_select_fusion.2), channel_id=1, source_target_pairs={{0,2},{2,0},{1,3},{3,1},{4,6},{6,4},{5,7},{7,5},{8,10},{10,8},{9,1... | collective-permute-start | bytes 1916936 | tf_op jit(solution)/shard_map/ppermute | solution.py:1031
  56.5 76.4 %copy-start.4 = (bf16[1536,768]{1,0:T(8,128)(2,1)}, bf16[1536,768]{1,0:T(8,128)(2,1)S(1)}, u32[]{:S(2)}) copy-start(bf16[1536,768]{1,0:T(8,128)(2,1)S(1)} %convert_bitcast_fusion.refs_3_) | copy-start | bytes 7077892
  60.0 21.8 %copy-start.22 = (bf16[2,2,2,24,1536]{4,3,2,1,0:T(8,128)(2,1)S(1)}, bf16[2,2,2,24,1536]{4,3,2,1,0:T(8,128)(2,1)}, u32[]{:S(2)}) copy-start(bf16[2,2,2,24,1536]{4,3,2,1,0:T(8,128)(2,1)} %broadcast_select_fusion.4) | copy-start | bytes 1769476
  62.5 20.5 %copy-start.6 = (bf16[768,1536]{1,0:T(8,128)(2,1)S(1)}, bf16[768,1536]{1,0:T(8,128)(2,1)}, u32[]{:S(2)}) copy-start(bf16[768,1536]{1,0:T(8,128)(2,1)} %copy-done.5) | copy-start | bytes 7077892
  62.5 19.3 %collective-permute-start.4 = (bf16[2,2,2,24,1536]{4,3,2,1,0:T(8,128)(2,1)}, bf16[2,2,2,24,1536]{4,3,2,1,0:T(8,128)(2,1)S(1)}, u32[]{:S(2)}, u32[]{:S(2)}) collective-permute-start(bf16[2,2,2,24,1536]{4,3,2,1,0:T(8,128)(2,1)} %broadcast_select_fusion.4), channel_id=1, source_target_pairs={{0,2},{2,0},{1,3},{3,1},{4,6},{6,4},{5,7},{7,5},{8,10},{10,8},{9,1... | collective-permute-start | bytes 1769480 | tf_op jit(solution)/shard_map/ppermute | solution.py:1031
  72.2 27.1 %collective-permute-start.8 = (bf16[2,2,2,2,24,1664]{5,4,3,2,1,0:T(8,128)(2,1)}, bf16[2,2,2,2,24,1664]{5,4,3,2,1,0:T(8,128)(2,1)}, u32[]{:S(2)}, u32[]{:S(2)}) collective-permute-start(bf16[2,2,2,2,24,1664]{5,4,3,2,1,0:T(8,128)(2,1)} %broadcast_select_fusion), channel_id=1, source_target_pairs={{0,1},{1,0},{2,3},{3,2},{4,5},{5,4},{6,7},{7,6},{8,9},{9,8},{10,11... | collective-permute-start | bytes 3833864 | tf_op jit(solution)/shard_map/ppermute | solution.py:1031
  83.0 12.9 %collective-permute-start.5 = (bf16[2,2,2,2,24,1536]{5,4,3,2,1,0:T(8,128)(2,1)}, bf16[2,2,2,2,24,1536]{5,4,3,2,1,0:T(8,128)(2,1)}, u32[]{:S(2)}, u32[]{:S(2)}) collective-permute-start(bf16[2,2,2,2,24,1536]{5,4,3,2,1,0:T(8,128)(2,1)} %broadcast_select_fusion.1), channel_id=1, source_target_pairs={{0,1},{1,0},{2,3},{3,2},{4,5},{5,4},{6,7},{7,6},{8,9},{9,8},{10,11... | collective-permute-start | bytes 3538952 | tf_op jit(solution)/shard_map/ppermute | solution.py:1031
  84.1 42.9 %collective-permute-start.10 = (bf16[384,1536]{1,0:T(8,128)(2,1)}, bf16[384,1536]{1,0:T(8,128)(2,1)S(1)}, u32[]{:S(2)}, u32[]{:S(2)}) collective-permute-start(bf16[384,1536]{1,0:T(8,128)(2,1)} %slice.70), channel_id=1, source_target_pairs={{0,2},{2,0},{1,3},{3,1},{4,6},{6,4},{5,7},{7,5},{8,10},{10,8},{9,1... | collective-permute-start | bytes 3538952 | tf_op jit(solution)/shard_map/ppermute | solution.py:1105
  86.6 40.5 %collective-permute-start.11 = (bf16[432,768]{1,0:T(8,128)(2,1)}, bf16[432,768]{1,0:T(8,128)(2,1)}, u32[]{:S(2)}, u32[]{:S(2)}) collective-permute-start(bf16[432,768]{1,0:T(8,128)(2,1)} %slice.71), channel_id=1, source_target_pairs={{0,2},{2,0},{1,3},{3,1},{4,6},{6,4},{5,7},{7,5},{8,10},{10,8},{9,1... | collective-permute-start | bytes 1990664 | tf_op jit(solution)/shard_map/ppermute | solution.py:1105
  127.1 7.1 %copy-start.16 = (bf16[384,1536]{1,0:T(8,128)(2,1)}, bf16[384,1536]{1,0:T(8,128)(2,1)S(1)}, u32[]{:S(2)}) copy-start(bf16[384,1536]{1,0:T(8,128)(2,1)S(1)} %collective-permute-done.10) | copy-start | bytes 3538948
  127.1 46.6 %all-to-all-start.1 = ((bf16[16,64,768]{2,1,0:T(8,128)(2,1)}), bf16[16,64,768]{2,1,0:T(8,128)(2,1)}, u32[]{:S(2)}, u32[]{:S(2)}) async-start(bf16[16,64,768]{2,1,0:T(8,128)(2,1)} %bitcast.92), calls=%async_computation.1 | async-start | bytes 3145728 | tf_op jit(solution)/shard_map/all_to_all | solution.py:1006
  134.2 39.5 %collective-permute-start.12 = (bf16[1104,768]{1,0:T(8,128)(2,1)}, bf16[1104,768]{1,0:T(8,128)(2,1)S(1)}, u32[]{:S(2)}, u32[]{:S(2)}) collective-permute-start(bf16[1104,768]{1,0:T(8,128)(2,1)} %slice.72), channel_id=1, source_target_pairs={{0,2},{2,0},{1,3},{3,1},{4,6},{6,4},{5,7},{7,5},{8,10},{10,8},{9,1... | collective-permute-start | bytes 5087240 | tf_op jit(solution)/shard_map/ppermute | solution.py:1105
  173.7 40.1 %all-to-all-start.2 = ((bf16[16,64,768]{2,1,0:T(8,128)(2,1)}), bf16[16,64,768]{2,1,0:T(8,128)(2,1)S(1)}, u32[]{:S(2)}, u32[]{:S(2)}) async-start(bf16[16,64,768]{2,1,0:T(8,128)(2,1)} %bitcast.91), calls=%async_computation.2 | async-start | bytes 3145728 | tf_op jit(solution)/shard_map/all_to_all | solution.py:1006
  213.8 7.2 %copy-start.11 = (bf16[16,64,768]{2,1,0:T(8,128)(2,1)}, bf16[16,64,768]{2,1,0:T(8,128)(2,1)S(1)}, u32[]{:S(2)}) copy-start(bf16[16,64,768]{2,1,0:T(8,128)(2,1)S(1)} %all-to-all-done.2) | copy-start | bytes 4718596
  213.8 41.5 %all-to-all-start.4 = ((bf16[16,64,768]{2,1,0:T(8,128)(2,1)}), bf16[16,64,768]{2,1,0:T(8,128)(2,1)S(1)}, u32[]{:S(2)}, u32[]{:S(2)}) async-start(bf16[16,64,768]{2,1,0:T(8,128)(2,1)} %get-tuple-element.98), calls=%async_computation.4 | async-start | bytes 3145728 | tf_op jit(solution)/shard_map/all_to_all | solution.py:1006
  255.3 24.5 %copy-start.24 = (bf16[16,64,768]{2,1,0:T(8,128)(2,1)}, bf16[16,64,768]{2,1,0:T(8,128)(2,1)S(1)}, u32[]{:S(2)}) copy-start(bf16[16,64,768]{2,1,0:T(8,128)(2,1)S(1)} %all-to-all-done.4) | copy-start | bytes 4718596
  255.3 47.0 %all-to-all-start.5 = ((bf16[16,64,768]{2,1,0:T(8,128)(2,1)}), bf16[16,64,768]{2,1,0:T(8,128)(2,1)S(1)}, u32[]{:S(2)}, u32[]{:S(2)}) async-start(bf16[16,64,768]{2,1,0:T(8,128)(2,1)} %get-tuple-element.89._early), calls=%async_computation.5 | async-start | bytes 3145728 | tf_op jit(solution)/shard_map/all_to_all | solution.py:1006
  279.9 22.4 %collective-permute-start.13 = (bf16[288,1536]{1,0:T(8,128)(2,1)}, bf16[288,1536]{1,0:T(8,128)(2,1)}, u32[]{:S(2)}, u32[]{:S(2)}) collective-permute-start(bf16[288,1536]{1,0:T(8,128)(2,1)} %bitcast.100), channel_id=1, source_target_pairs={{0,2},{2,0},{1,3},{3,1},{4,6},{6,4},{5,7},{7,5},{8,10},{10,8},{9,1... | collective-permute-start | bytes 2654216 | tf_op jit(solution)/shard_map/ppermute | solution.py:1108
  303.5 65.1 %all-to-all-start.3 = ((bf16[16,128,768]{2,1,0:T(8,128)(2,1)}), bf16[16,128,768]{2,1,0:T(8,128)(2,1)S(1)}, u32[]{:S(2)}, u32[]{:S(2)}) async-start(bf16[16,128,768]{2,1,0:T(8,128)(2,1)} %get-tuple-element.93), calls=%async_computation.3 | async-start | bytes 6291456 | tf_op jit(solution)/shard_map/all_to_all | solution.py:1006
  309.2 51.7 %collective-permute-start.14 = (bf16[480,1536]{1,0:T(8,128)(2,1)}, bf16[480,1536]{1,0:T(8,128)(2,1)S(1)}, u32[]{:S(2)}, u32[]{:S(2)}) collective-permute-start(bf16[480,1536]{1,0:T(8,128)(2,1)} %bitcast.99), channel_id=1, source_target_pairs={{0,2},{2,0},{1,3},{3,1},{4,6},{6,4},{5,7},{7,5},{8,10},{10,8},{9,1... | collective-permute-start | bytes 4423688 | tf_op jit(solution)/shard_map/ppermute | solution.py:1108
  310.8 50.1 %collective-permute-start.15 = (bf16[1536,256]{1,0:T(8,128)(2,1)}, bf16[1536,256]{1,0:T(8,128)(2,1)S(1)}, u32[]{:S(2)}, u32[]{:S(2)}) collective-permute-start(bf16[1536,256]{1,0:T(8,128)(2,1)} %bitcast.101), channel_id=1, source_target_pairs={{0,2},{2,0},{1,3},{3,1},{4,6},{6,4},{5,7},{7,5},{8,10},{10,8},{9,1... | collective-permute-start | bytes 2359304 | tf_op jit(solution)/shard_map/ppermute | solution.py:1108
  360.9 4.0 collective-permute-start.16
  361.0 23.0 %collective-permute-start.18 = (bf16[2,8,24,1664]{3,2,1,0:T(8,128)(2,1)}, bf16[2,8,24,1664]{3,2,1,0:T(8,128)(2,1)}, u32[]{:S(2)}, u32[]{:S(2)}) collective-permute-start(bf16[2,8,24,1664]{3,2,1,0:T(8,128)(2,1)} %get-tuple-element.115), channel_id=1, source_target_pairs={{0,1},{1,0},{2,3},{3,2},{4,5},{5,4},{6,7},{7,6},{8,9},{9,8},{10,11... | collective-permute-start | bytes 3833864 | tf_op jit(solution)/shard_map/ppermute | solution.py:1232
  361.5 36.7 %collective-permute-start.19 = (bf16[1536,512]{1,0:T(8,128)(2,1)}, bf16[1536,512]{1,0:T(8,128)(2,1)}, u32[]{:S(2)}, u32[]{:S(2)}) collective-permute-start(bf16[1536,512]{1,0:T(8,128)(2,1)} %bitcast.98), channel_id=1, source_target_pairs={{0,2},{2,0},{1,3},{3,1},{4,6},{6,4},{5,7},{7,5},{8,10},{10,8},{9,1... | collective-permute-start | bytes 4718600 | tf_op jit(solution)/shard_map/ppermute | solution.py:1108
  368.6 47.6 %all-to-all-start.6 = ((bf16[8,2,24,1536]{3,2,1,0:T(8,128)(2,1)}), bf16[8,2,24,1536]{3,2,1,0:T(8,128)(2,1)}, u32[]{:S(2)}, u32[]{:S(2)}) async-start(bf16[8,2,24,1536]{3,2,1,0:T(8,128)(2,1)} %convert_add_fusion.2), calls=%async_computation.6 | async-start | bytes 2359296 | tf_op jit(solution)/shard_map/all_to_all | solution.py:1242
  386.1 12.1 %copy-start.14 = (bf16[2,8,24,1664]{3,2,1,0:T(8,128)(2,1)}, bf16[2,8,24,1664]{3,2,1,0:T(8,128)(2,1)S(1)}, u32[]{:S(2)}) copy-start(bf16[2,8,24,1664]{3,2,1,0:T(8,128)(2,1)S(1)} %add_convert_fusion) | copy-start | bytes 3833860
  398.2 15.7 %collective-permute-start.20 = (bf16[8,24,1664]{2,1,0:T(8,128)(2,1)S(1)}, bf16[8,24,1664]{2,1,0:T(8,128)(2,1)}, u32[]{:S(2)}, u32[]{:S(2)}) collective-permute-start(bf16[8,24,1664]{2,1,0:T(8,128)(2,1)S(1)} %dynamic-slice_bitcast_fusion), channel_id=1, source_target_pairs={{0,2},{2,0},{1,3},{3,1},{4,6},{6,4},{5,7},{7,5},{8,10},{10,8},{9,1... | collective-permute-start | bytes 1916936 | tf_op jit(solution)/shard_map/ppermute | solution.py:1048
  408.0 15.6 %copy-start.7 = (bf16[768,1536]{1,0:T(8,128)(2,1)S(1)}, bf16[768,1536]{1,0:T(8,128)(2,1)}, u32[]{:S(2)}) copy-start(bf16[768,1536]{1,0:T(8,128)(2,1)} %get-tuple-element.91._early) | copy-start | bytes 7077892
  417.6 21.3 %all-to-all-start.7 = ((bf16[8,24,1664]{2,1,0:T(8,128)(2,1)}), bf16[8,24,1664]{2,1,0:T(8,128)(2,1)S(1)}, u32[]{:S(2)}, u32[]{:S(2)}) async-start(bf16[8,24,1664]{2,1,0:T(8,128)(2,1)} %convert_add_fusion.3), calls=%async_computation.7 | async-start | bytes 1277952 | tf_op jit(solution)/shard_map/all_to_all | solution.py:1242
  427.2 31.7 %copy-start.26 = (f32[24,16]{0,1:T(8,128)S(1)}, f32[24,16]{0,1:T(8,128)}, u32[]{:S(2)}) copy-start(f32[24,16]{0,1:T(8,128)} %param.29) | copy-start | bytes 4612
  427.2 31.7 %copy-start.27 = (f32[24,16]{0,1:T(8,128)S(1)}, f32[24,16]{0,1:T(8,128)}, u32[]{:S(2)}) copy-start(f32[24,16]{0,1:T(8,128)} %param.39) | copy-start | bytes 4612
  427.2 31.7 %copy-start.28 = (f32[24,16]{0,1:T(8,128)S(1)}, f32[24,16]{0,1:T(8,128)}, u32[]{:S(2)}) copy-start(f32[24,16]{0,1:T(8,128)} %param.38) | copy-start | bytes 4612
  427.2 4.8 collective-permute-start.17
  432.0 29.6 %copy-start.29 = (f32[24,4]{0,1:T(4,128)S(1)}, f32[24,4]{0,1:T(4,128)}, u32[]{:S(2)}) copy-start(f32[24,4]{0,1:T(4,128)} %param.26) | copy-start | bytes 1156
  432.0 29.6 %copy-start.32 = (f32[24,4]{0,1:T(4,128)S(1)}, f32[24,4]{0,1:T(4,128)}, u32[]{:S(2)}) copy-start(f32[24,4]{0,1:T(4,128)} %param.33) | copy-start | bytes 1156
  438.9 35.3 %slice-start.1 = ((s8[4718592]{0:T(1024)(128)(4,1)}), s8[524288]{0:T(1024)(128)(4,1)S(1)}, s32[]{:S(2)}) async-start(s8[4718592]{0:T(1024)(128)(4,1)} %bitcast.74), calls=%async_computation.10 | async-start | bytes 1048576
  443.9 10.8 %all-to-all-start.8 = ((f32[32,1,128]{2,1,0:T(1,128)}), f32[32,1,128]{2,1,0:T(1,128)S(1)}, u32[]{:S(2)}, u32[]{:S(2)}) async-start(f32[32,1,128]{2,1,0:T(1,128)} %broadcast_in_dim.259), calls=%async_computation.8 | async-start | bytes 32768 | tf_op jit(solution)/shard_map/all_to_all | solution.py:1262
  462.9 11.4 %slice-start.2 = ((s8[4718592]{0:T(1024)(128)(4,1)}), s8[4194304]{0:T(1024)(128)(4,1)S(1)}, s32[]{:S(2)}) async-start(s8[4718592]{0:T(1024)(128)(4,1)} %bitcast.74), calls=%async_computation.11 | async-start | bytes 8388608
  462.9 12.1 %copy-start.13 = (bf16[480,1536]{1,0:T(8,128)(2,1)S(1)}, bf16[480,1536]{1,0:T(8,128)(2,1)}, u32[]{:S(2)}) copy-start(bf16[480,1536]{1,0:T(8,128)(2,1)} %copy-done.12) | copy-start | bytes 4423684
  (18 other events, 59.8 us)

commit v2 on v1

--- a/solution.py
+++ b/solution.py
@@ -593,7 +593,7 @@
     wide_spec = lambda first: pl.BlockSpec((chunk, block), lambda s: (0, first + s))
     wide_specs = [wide_spec(per_ring if far and whole else 0) for _array, whole in wides]
     if far:
-        in_cuts, out_cuts = (width * 3 // 8, width * 5 // 8), (width // 3, width - width // 3)
+        in_cuts = out_cuts = (width // 3, width - width // 3)
         out_specs = [
             pl.BlockSpec((None, part, block), lambda s: (s // per_ring, 0, s % per_ring))
             for part in in_cuts

time: 494 us -> 493 us (level)
  transfers between devices with their start and end apart: 30 -> 30, of which waited for: 15 -> 14; matrix products, arithmetic and copies ran while one was open for 14% -> 14% of each run, Pallas kernels for 39% -> 39%
where the time goes in v2:
time: 493 us; the launch traced here: 485 us
  Pallas kernels  191 us (39%)
  waiting for transfers between devices  95 us (19%)
  starting transfers between devices  85.1 us (17%)
  other arithmetic  66.4 us (13%)
  local copies, waits for them, and re-layouts  42.5 us (9%)
  between operations  5.39 us (1%)
    pallas_call x2, Pallas kernels, call_experts(): pl.pallas_call(functools.partial(expert_kernel, sz, ring, per_ring, bool(...  68.7 us
    all_to_all x6, starting transfers between devices, exchange(): return lax.all_to_all(array, GROUP, split_axis=0, concat_axis=0, tiled=True)  36.5 us
    pallas_call x2, Pallas kernels, call_weight_grads(): pl.pallas_call(weight_grad_kernel, grid=(count,), in_specs=[flat_spec] *...  35.3 us
    ppermute x5, waiting for transfers between devices, from_ahead(): lax.ppermute(array, 'row', [(s, (s - r) % ring) for s in range(ring)])  35 us
    pallas_call x1, Pallas kernels, call_attend_back(): pl.pallas_call(functools.partial(attend_back_kernel, sz), grid=(images,),...  28.8 us
    ppermute x8, waiting for transfers between devices, double(): lax.ppermute(array, axis, [(s, s ^ flip) for s in range(lax.axis_size(axi...  28 us
    sub x6, other arithmetic, adam_update(): weight - rate_val * (first_hat / (jnp.sqrt(second_hat) + ADAM_EPS) + deca...  26.1 us
    pallas_call x1, Pallas kernels, call_attend(): pl.pallas_call(functools.partial(attend_kernel, sz), grid=(images,), in_s...  24 us
  transfers between devices with their start and end apart: 30, of which 14 were waited for; matrix products, arithmetic and copies ran while one was open for 14% of the time, Pallas kernels for 39%

profile of v2, /device:TPU:0, one launch (start us, length us, event | category | flops | bytes accessed | tf_op | source)
XLA Modules:
  0.0 485.5 jit_solution(6013073389583446521)
XLA Ops:
  4.2 4.1 collective-permute-start
  8.3 2.6 convert_bitcast_fusion.1.refs_2_
  19.0 10.5 %slots.1 = (s32[8,896]{1,0:T(8,128)}, bf16[16,128,768]{2,1,0:T(8,128)(2,1)}) custom-call(s32[1,1792]{1,0:T(1,128)} %reshape.159.order_ref, s32[1,1792]{1,0:T(1,128)} %bitcast.96, bf16[896,768]{1,0:T(8,128)(2,1)} %pad.34.dy_ref), custom_call_target="tpu_custom_call" | custom-call | flops 1024 | bytes 1024 | tf_op jit(solution)/shard_map/slots/pallas_call | solution.py:176
  33.5 6.4 %collective-permute-done.3 = bf16[2,2,24,1536]{3,2,1,0:T(8,128)(2,1)S(1)} collective-permute-done((bf16[2,2,24,1536]{3,2,1,0:T(8,128)(2,1)S(1)}, bf16[2,2,24,1536]{3,2,1,0:T(8,128)(2,1)S(1)}, u32[]{:S(2)}, u32[]{:S(2)}) %collective-permute-start.3) | collective-permute-done | bytes 294944 | tf_op jit(solution)/shard_map/ppermute | solution.py:1031
  40.8 4.6 collective-permute-done.6
  47.1 5.3 %all-to-all-start = ((bf16[16,128,768]{2,1,0:T(8,128)(2,1)}), bf16[16,128,768]{2,1,0:T(8,128)(2,1)}, u32[]{:S(2)}, u32[]{:S(2)}) async-start(bf16[16,128,768]{2,1,0:T(8,128)(2,1)} %get-tuple-element.76), calls=%async_computation | async-start | bytes 6291456 | tf_op jit(solution)/shard_map/all_to_all | solution.py:1006
  53.9 2.6 convert_bitcast_fusion.refs_3_
  56.5 3.5 reshape.157
  60.0 2.5 pad.31.tok_ref
  63.0 6.7 %collective-permute-done.7 = bf16[2,2,2,24,1664]{4,3,2,1,0:T(8,128)(2,1)} collective-permute-done((bf16[2,2,2,24,1664]{4,3,2,1,0:T(8,128)(2,1)S(1)}, bf16[2,2,2,24,1664]{4,3,2,1,0:T(8,128)(2,1)}, u32[]{:S(2)}, u32[]{:S(2)}) %collective-permute-start.7) | collective-permute-done | bytes 639008 | tf_op jit(solution)/shard_map/ppermute | solution.py:1031
  69.7 2.5 broadcast_select_fusion
  72.2 9.7 %collective-permute-done.4 = bf16[2,2,2,24,1536]{4,3,2,1,0:T(8,128)(2,1)S(1)} collective-permute-done((bf16[2,2,2,24,1536]{4,3,2,1,0:T(8,128)(2,1)}, bf16[2,2,2,24,1536]{4,3,2,1,0:T(8,128)(2,1)S(1)}, u32[]{:S(2)}, u32[]{:S(2)}) %collective-permute-start.4) | collective-permute-done | bytes 589856 | tf_op jit(solution)/shard_map/ppermute | solution.py:1031
  90.9 1.8 pad.35.clone
  95.9 3.3 bitcast_select_fusion.1.w_one_ref
  99.2 3.7 bitcast_select_fusion.w_two_ref.proj_ref.tail_ref
  103.0 24.0 %attend.1 = (bf16[4,224,2304]{2,1,0:T(8,128)(2,1)}, f32[4,16,224]{2,1,0:T(8,128)}, bf16[4,224,768]{2,1,0:T(8,128)(2,1)}, f32[4,224,768]{2,1,0:T(8,128)}, bf16[4,...) custom-call(bf16[4,224,768]{2,1,0:T(8,128)(2,1)} %pad.31.tok_ref, ...), custom_call_target="tpu_custom_call" | custom-call | flops 1024 | bytes 1024 | tf_op jit(solution)/shard_map/attend/pallas_call | solution.py:307
  127.0 5.8 %all-to-all-start.1 = ((bf16[16,64,768]{2,1,0:T(8,128)(2,1)}), bf16[16,64,768]{2,1,0:T(8,128)(2,1)}, u32[]{:S(2)}, u32[]{:S(2)}) async-start(bf16[16,64,768]{2,1,0:T(8,128)(2,1)} %bitcast.92), calls=%async_computation.1 | async-start | bytes 3145728 | tf_op jit(solution)/shard_map/all_to_all | solution.py:1006
  139.4 34.3 %collective-permute-done.12 = bf16[1104,768]{1,0:T(8,128)(2,1)S(1)} collective-permute-done((bf16[1104,768]{1,0:T(8,128)(2,1)}, bf16[1104,768]{1,0:T(8,128)(2,1)S(1)}, u32[]{:S(2)}, u32[]{:S(2)}) %collective-permute-start.12) | collective-permute-done | bytes 1695776 | tf_op jit(solution)/shard_map/ppermute | solution.py:1105
  173.7 5.8 %all-to-all-start.2 = ((bf16[16,64,768]{2,1,0:T(8,128)(2,1)}), bf16[16,64,768]{2,1,0:T(8,128)(2,1)S(1)}, u32[]{:S(2)}, u32[]{:S(2)}) async-start(bf16[16,64,768]{2,1,0:T(8,128)(2,1)} %bitcast.91), calls=%async_computation.2 | async-start | bytes 3145728 | tf_op jit(solution)/shard_map/all_to_all | solution.py:1006
  179.4 34.3 %experts.2 = (bf16[1024,3072]{1,0:T(8,128)(2,1)}, bf16[1024,3072]{1,0:T(8,128)(2,1)}, bf16[1024,768]{1,0:T(8,128)(2,1)}, bf16[16,128,768]{2,1,0:T(8,128)(2,1)}, bf16[16,64,768]{2,1,0:T(8,128)(2,1)}) custom-call(bf16[1024,768]{1,0:T(8,128)(2,1)} %bitcast.13.refs_0_.x_one, bf16[16,128,768]{2,1,0:T(8,128)(2,1)} %all-to-all-done.refs_1_, ...), custom_call_target="tpu_custom_call" | custom-call | flops 1024 | bytes 1024 | tf_op jit(solution)/shard_map/experts/pallas_call | solution.py:534
  213.8 7.1 %all-to-all-start.4 = ((bf16[16,64,768]{2,1,0:T(8,128)(2,1)}), bf16[16,64,768]{2,1,0:T(8,128)(2,1)S(1)}, u32[]{:S(2)}, u32[]{:S(2)}) async-start(bf16[16,64,768]{2,1,0:T(8,128)(2,1)} %get-tuple-element.98), calls=%async_computation.4 | async-start | bytes 3145728 | tf_op jit(solution)/shard_map/all_to_all | solution.py:1006
  221.0 34.4 %experts.3 = (bf16[1024,3072]{1,0:T(8,128)(2,1)}, bf16[1024,3072]{1,0:T(8,128)(2,1)}, bf16[1024,768]{1,0:T(8,128)(2,1)}, bf16[16,128,768]{2,1,0:T(8,128)(2,1)}, bf16[16,64,768]{2,1,0:T(8,128)(2,1)}) custom-call(bf16[1024,768]{1,0:T(8,128)(2,1)} %bitcast.78, bf16[16,128,768]{2,1,0:T(8,128)(2,1)} %all-to-all-done.refs_1_, ...), custom_call_target="tpu_custom_call", output_to_operand_aliasing={{3}: (9, {})} | custom-call | flops 1024 | bytes 1024 | tf_op jit(solution)/shard_map/experts/pallas_call | solution.py:534
  255.3 6.8 %all-to-all-start.5 = ((bf16[16,64,768]{2,1,0:T(8,128)(2,1)}), bf16[16,64,768]{2,1,0:T(8,128)(2,1)S(1)}, u32[]{:S(2)}, u32[]{:S(2)}) async-start(bf16[16,64,768]{2,1,0:T(8,128)(2,1)} %get-tuple-element.89._early), calls=%async_computation.5 | async-start | bytes 3145728 | tf_op jit(solution)/shard_map/all_to_all | solution.py:1006
  262.2 17.7 %weight_grads.2 = (bf16[1,256,1536]{2,1,0:T(8,128)(2,1)}, bf16[1,512,1536]{2,1,0:T(8,128)(2,1)}, bf16[1,1536,256]{2,1,0:T(8,128)(2,1)}, bf16[1,1536,512]{2,1,0:T(8,128)(2,1)}) custom-call(bf16[1024,768]{1,0:T(8,128)(2,1)} %bitcast.13.refs_0_.x_one, bf16[1024,768]{1,0:T(8,128)(2,1)} %bitcast.79, bf16[1024,768]{1,0:T(8,128)(2,1)} %get-tuple-element.83.grad_one, ...), custom_call_target="tpu_custom_call" | custom-call | flops 9663676416 | bytes 22020096 | tf_op jit(solution)/shard_map/weight_grads/pallas_call | solution.py:616
  281.5 17.6 %weight_grads.3 = (bf16[768,1536]{1,0:T(8,128)(2,1)}, bf16[1536,768]{1,0:T(8,128)(2,1)}) custom-call(bf16[1024,768]{1,0:T(8,128)(2,1)} %bitcast.13.refs_0_.x_one, bf16[1024,768]{1,0:T(8,128)(2,1)} %bitcast.80, bf16[1024,768]{1,0:T(8,128)(2,1)} %get-tuple-element.83.grad_one, bf16[1024,768]{1,0:T(8,128)(2,1)} %get-tuple-element.84.grad_two, ...), custom_call_target="tpu_custom_call" | custom-call | flops 9663676416 | bytes 22020096 | tf_op jit(solution)/shard_map/weight_grads/pallas_call | solution.py:616
  301.4 5.8 %all-to-all-start.3 = ((bf16[16,128,768]{2,1,0:T(8,128)(2,1)}), bf16[16,128,768]{2,1,0:T(8,128)(2,1)S(1)}, u32[]{:S(2)}, u32[]{:S(2)}) async-start(bf16[16,128,768]{2,1,0:T(8,128)(2,1)} %get-tuple-element.93), calls=%async_computation.3 | async-start | bytes 6291456 | tf_op jit(solution)/shard_map/all_to_all | solution.py:1006
  309.2 17.2 %combine.1 = (f32[4,224,768]{2,1,0:T(8,128)}, bf16[4,224,768]{2,1,0:T(8,128)(2,1)}, bf16[768,768]{1,0:T(8,128)(2,1)}, f32[128,768]{1,0:T(8,128)}) custom-call(bf16[1024,768]{1,0:T(8,128)(2,1)} %bitcast.89, bf16[1024,768]{1,0:T(8,128)(2,1)} %bitcast.90, s32[8,896]{1,0:T(8,128)} %copy.196.slot_ref, s32[896,128]{1,0:T(8,128)} %pad.38.slot_col_ref, ...), custom_call_target="tpu_custom_call" | custom-call | flops 4932501504 | bytes 16515072 | tf_op jit(solution)/shard_map/combine/pallas_call | solution.py:749
  326.4 28.8 %attend_back.1 = (f32[4,224,768]{2,1,0:T(8,128)}, bf16[8,2,24,1536]{3,2,1,0:T(8,128)(2,1)}, bf16[8,2,24,1536]{3,2,1,0:T(8,128)(2,1)}, bf16[2,8,24,1664]{3,2,1,0:T(8,128)(2,1)}, bf16[2,8,24,1664]{3,2,1,0:T(8,128)(2,1)}) custom-call(bf16[4,224,768]{2,1,0:T(8,128)(2,1)} %pad.31.tok_ref, bf16[768,1536]{1,0:T(8,128)(2,1)} %bitcast_select_fusion.1.w_one_ref, ...), custom_call_target="tpu_custom_call" | custom-call | flops 7883194368 | bytes 22216704 | tf_op jit(solution)/shard_map/attend_back/pallas_call | solution.py:918
  355.2 5.7 %collective-permute-done.15 = bf16[1536,256]{1,0:T(8,128)(2,1)S(1)} collective-permute-done((bf16[1536,256]{1,0:T(8,128)(2,1)}, bf16[1536,256]{1,0:T(8,128)(2,1)S(1)}, u32[]{:S(2)}, u32[]{:S(2)}) %collective-permute-start.15) | collective-permute-done | bytes 786464 | tf_op jit(solution)/shard_map/ppermute | solution.py:1108
  363.0 1.9 collective-permute-done.16
  364.9 2.7 convert_add_fusion.2
  367.6 14.2 %all-to-all-start.6 = ((bf16[8,2,24,1536]{3,2,1,0:T(8,128)(2,1)}), bf16[8,2,24,1536]{3,2,1,0:T(8,128)(2,1)}, u32[]{:S(2)}, u32[]{:S(2)}) async-start(bf16[8,2,24,1536]{3,2,1,0:T(8,128)(2,1)} %convert_add_fusion.2), calls=%async_computation.6 | async-start | bytes 2359296 | tf_op jit(solution)/shard_map/all_to_all | solution.py:1242
  381.9 2.1 add_convert_fusion
  384.6 6.6 %output.1 = bf16[4,224,768]{2,1,0:T(8,128)(2,1)S(1)} custom-call(bf16[16,128,768]{2,1,0:T(8,128)(2,1)S(1)} %all-to-all-done.3.res_ref, s32[896,128]{1,0:T(8,128)S(1)} %copy-done.2, f32[896,128]{1,0:T(8,128)S(1)} %copy-done.3, f32[4,224,768]{2,1,0:T(8,128)S(1)} %copy-done.1), custom_call_target="tpu_custom_call" | custom-call | flops 1024 | bytes 1024 | tf_op jit(solution)/shard_map/output/pallas_call | solution.py:975
  392.3 5.9 %collective-permute-done.19 = bf16[1536,512]{1,0:T(8,128)(2,1)} collective-permute-done((bf16[1536,512]{1,0:T(8,128)(2,1)}, bf16[1536,512]{1,0:T(8,128)(2,1)}, u32[]{:S(2)}, u32[]{:S(2)}) %collective-permute-start.19) | collective-permute-done | bytes 1572896 | tf_op jit(solution)/shard_map/ppermute | solution.py:1108
  399.8 3.3 slice.62
  403.1 3.5 reshape.172
  408.0 6.0 %collective-permute-done.20 = bf16[8,24,1664]{2,1,0:T(8,128)(2,1)} collective-permute-done((bf16[8,24,1664]{2,1,0:T(8,128)(2,1)S(1)}, bf16[8,24,1664]{2,1,0:T(8,128)(2,1)}, u32[]{:S(2)}, u32[]{:S(2)}) %collective-permute-start.20) | collective-permute-done | bytes 639008 | tf_op jit(solution)/shard_map/ppermute | solution.py:1048
  413.9 2.1 convert_add_fusion.3
  417.4 5.9 %all-to-all-start.7 = ((bf16[8,24,1664]{2,1,0:T(8,128)(2,1)}), bf16[8,24,1664]{2,1,0:T(8,128)(2,1)S(1)}, u32[]{:S(2)}, u32[]{:S(2)}) async-start(bf16[8,24,1664]{2,1,0:T(8,128)(2,1)} %convert_add_fusion.3), calls=%async_computation.7 | async-start | bytes 1277952 | tf_op jit(solution)/shard_map/all_to_all | solution.py:1242
  423.4 4.3 multiply_reduce_fusion
  429.3 3.0 multiply_reduce_fusion.1
  432.9 5.8 %all-to-all-done.7 = bf16[8,24,1664]{2,1,0:T(8,128)(2,1)S(1)} async-done(((bf16[8,24,1664]{2,1,0:T(8,128)(2,1)}), bf16[8,24,1664]{2,1,0:T(8,128)(2,1)S(1)}, u32[]{:S(2)}, u32[]{:S(2)}) %all-to-all-start.7) | async-done | bytes 639008 | tf_op jit(solution)/shard_map/all_to_all | solution.py:1242
  443.7 3.7 all-to-all-start.8
  449.1 5.4 %all-to-all-done.8 = f32[32,1,128]{2,1,0:T(1,128)S(1)} async-done(((f32[32,1,128]{2,1,0:T(1,128)}), f32[32,1,128]{2,1,0:T(1,128)S(1)}, u32[]{:S(2)}, u32[]{:S(2)}) %all-to-all-start.8) | async-done | bytes 16416 | tf_op jit(solution)/shard_map/all_to_all | solution.py:1262
  459.3 2.1 multiply_subtract_fusion.2
  462.7 11.4 %multiply_subtract_fusion = (f32[1,1536,768]{2,1,0:T(8,128)}, f32[1,1536,768]{2,1,0:T(8,128)}, f32[1,1536,768]{2,1,0:T(8,128)}) fusion(f32[1,1536,768]{2,1,0:T(8,128)} %param.31, f32[]{:T(128)S(6)} %min.3, bf16[1536,512]{1,0:T(8,128)(2,1)} %collective-permute-done.19, bf16[1536,256]{1,0:T(8,128)(2,1)} %copy-done.19, bf16[1536,768]{1,0:T(8,128)(2,1)S(1)} %copy-done.8, ...), kind=kLoop, calls=%fused_computation.8 | loop fusion | flops 25952256 | bytes 33030148 | tf_op jit(solution)/shard_map/sub | solution.py:1001
  474.9 9.0 %multiply_subtract_fusion.1 = (f32[1,768,1536]{2,1,0:T(8,128)}, f32[1,768,1536]{2,1,0:T(8,128)}, f32[1,768,1536]{2,1,0:T(8,128)}) fusion(f32[1,768,1536]{2,1,0:T(8,128)S(1)} %bitcast.75, f32[]{:T(128)S(6)} %min.3, bf16[512,1536]{1,0:T(8,128)(2,1)S(1)} %copy-done.12, bf16[256,1536]{1,0:T(8,128)(2,1)} %collective-permute-done.13, ...), kind=kLoop, calls=%fused_computation.9 | loop fusion | flops 25952256 | bytes 33030148 | tf_op jit(solution)/shard_map/sub | solution.py:1001
  (172 shorter events, 66.3 us)
Async XLA Ops:
  4.2 10.5 %copy-start.31 = (s32[1,1576]{1,0:T(1,128)S(1)}, s32[1,1576]{1,0:T(1,128)}, u32[]{:S(2)}) copy-start(s32[1,1576]{1,0:T(1,128)} %param.25) | copy-start | bytes 18916
  4.2 11.4 %collective-permute-start = (bf16[24,3200]{1,0:T(8,128)(2,1)S(1)}, bf16[24,3200]{1,0:T(8,128)(2,1)S(1)}, u32[]{:S(2)}, u32[]{:S(2)}) collective-permute-start(bf16[24,3200]{1,0:T(8,128)(2,1)S(1)} %concatenate.12), channel_id=1, source_target_pairs={{0,16},{4,20},{8,24},{12,28},{16,0},{20,4},{24,8},{28,12},{1,17},{... | collective-permute-start | bytes 460808 | tf_op jit(solution)/shard_map/ppermute | solution.py:1031
  13.2 16.6 %collective-permute-start.2 = (bf16[192,1536]{1,0:T(8,128)(2,1)S(1)}, bf16[192,1536]{1,0:T(8,128)(2,1)S(1)}, u32[]{:S(2)}, u32[]{:S(2)}) collective-permute-start(bf16[192,1536]{1,0:T(8,128)(2,1)S(1)} %get-tuple-element.264), channel_id=1, source_target_pairs={{0,2},{2,0},{1,3},{3,1},{4,6},{6,4},{5,7},{7,5},{8,10},{10,8},{9,1... | collective-permute-start | bytes 1769480 | tf_op jit(solution)/shard_map/ppermute | solution.py:1105
  15.7 13.8 %collective-permute-start.1 = (bf16[2,24,3200]{2,1,0:T(8,128)(2,1)S(1)}, bf16[2,24,3200]{2,1,0:T(8,128)(2,1)S(1)}, u32[]{:S(2)}, u32[]{:S(2)}) collective-permute-start(bf16[2,24,3200]{2,1,0:T(8,128)(2,1)S(1)} %broadcast_select_fusion.5), channel_id=1, source_target_pairs={{0,8},{4,12},{8,0},{12,4},{16,24},{20,28},{24,16},{28,20},{1,9},{5... | collective-permute-start | bytes 921608 | tf_op jit(solution)/shard_map/ppermute | solution.py:1031
  29.8 16.4 %copy-start.20 = (bf16[192,1536]{1,0:T(8,128)(2,1)}, bf16[192,1536]{1,0:T(8,128)(2,1)S(1)}, u32[]{:S(2)}) copy-start(bf16[192,1536]{1,0:T(8,128)(2,1)S(1)} %collective-permute-done.2) | copy-start | bytes 1769476
  29.9 10.0 %collective-permute-start.3 = (bf16[2,2,24,1536]{3,2,1,0:T(8,128)(2,1)S(1)}, bf16[2,2,24,1536]{3,2,1,0:T(8,128)(2,1)S(1)}, u32[]{:S(2)}, u32[]{:S(2)}) collective-permute-start(bf16[2,2,24,1536]{3,2,1,0:T(8,128)(2,1)S(1)} %slice.52), channel_id=1, source_target_pairs={{0,4},{4,0},{8,12},{12,8},{16,20},{20,16},{24,28},{28,24},{1,5},{5... | collective-permute-start | bytes 884744 | tf_op jit(solution)/shard_map/ppermute | solution.py:1031
  31.4 14.8 %collective-permute-start.9 = (bf16[192,1536]{1,0:T(8,128)(2,1)}, bf16[192,1536]{1,0:T(8,128)(2,1)S(1)}, u32[]{:S(2)}, u32[]{:S(2)}) collective-permute-start(bf16[192,1536]{1,0:T(8,128)(2,1)} %get-tuple-element.263), channel_id=1, source_target_pairs={{0,2},{2,0},{1,3},{3,1},{4,6},{6,4},{5,7},{7,5},{8,10},{10,8},{9,1... | collective-permute-start | bytes 1769480 | tf_op jit(solution)/shard_map/ppermute | solution.py:1105
  32.9 12.5 %collective-permute-start.6 = (bf16[2,2,24,1664]{3,2,1,0:T(8,128)(2,1)S(1)}, bf16[2,2,24,1664]{3,2,1,0:T(8,128)(2,1)S(1)}, u32[]{:S(2)}, u32[]{:S(2)}) collective-permute-start(bf16[2,2,24,1664]{3,2,1,0:T(8,128)(2,1)S(1)} %slice.53), channel_id=1, source_target_pairs={{0,4},{4,0},{8,12},{12,8},{16,20},{20,16},{24,28},{28,24},{1,5},{5... | collective-permute-start | bytes 958472 | tf_op jit(solution)/shard_map/ppermute | solution.py:1031
  47.1 80.0 %all-to-all-start = ((bf16[16,128,768]{2,1,0:T(8,128)(2,1)}), bf16[16,128,768]{2,1,0:T(8,128)(2,1)}, u32[]{:S(2)}, u32[]{:S(2)}) async-start(bf16[16,128,768]{2,1,0:T(8,128)(2,1)} %get-tuple-element.76), calls=%async_computation | async-start | bytes 6291456 | tf_op jit(solution)/shard_map/all_to_all | solution.py:1006
  52.4 17.3 %collective-permute-start.7 = (bf16[2,2,2,24,1664]{4,3,2,1,0:T(8,128)(2,1)S(1)}, bf16[2,2,2,24,1664]{4,3,2,1,0:T(8,128)(2,1)}, u32[]{:S(2)}, u32[]{:S(2)}) collective-permute-start(bf16[2,2,2,24,1664]{4,3,2,1,0:T(8,128)(2,1)S(1)} %broadcast_select_fusion.2), channel_id=1, source_target_pairs={{0,2},{2,0},{1,3},{3,1},{4,6},{6,4},{5,7},{7,5},{8,10},{10,8},{9,1... | collective-permute-start | bytes 1916936 | tf_op jit(solution)/shard_map/ppermute | solution.py:1031
  56.5 76.4 %copy-start.4 = (bf16[1536,768]{1,0:T(8,128)(2,1)}, bf16[1536,768]{1,0:T(8,128)(2,1)S(1)}, u32[]{:S(2)}) copy-start(bf16[1536,768]{1,0:T(8,128)(2,1)S(1)} %convert_bitcast_fusion.refs_3_) | copy-start | bytes 7077892
  60.0 21.8 %copy-start.22 = (bf16[2,2,2,24,1536]{4,3,2,1,0:T(8,128)(2,1)S(1)}, bf16[2,2,2,24,1536]{4,3,2,1,0:T(8,128)(2,1)}, u32[]{:S(2)}) copy-start(bf16[2,2,2,24,1536]{4,3,2,1,0:T(8,128)(2,1)} %broadcast_select_fusion.4) | copy-start | bytes 1769476
  62.5 20.5 %copy-start.6 = (bf16[768,1536]{1,0:T(8,128)(2,1)S(1)}, bf16[768,1536]{1,0:T(8,128)(2,1)}, u32[]{:S(2)}) copy-start(bf16[768,1536]{1,0:T(8,128)(2,1)} %copy-done.5) | copy-start | bytes 7077892
  62.5 19.3 %collective-permute-start.4 = (bf16[2,2,2,24,1536]{4,3,2,1,0:T(8,128)(2,1)}, bf16[2,2,2,24,1536]{4,3,2,1,0:T(8,128)(2,1)S(1)}, u32[]{:S(2)}, u32[]{:S(2)}) collective-permute-start(bf16[2,2,2,24,1536]{4,3,2,1,0:T(8,128)(2,1)} %broadcast_select_fusion.4), channel_id=1, source_target_pairs={{0,2},{2,0},{1,3},{3,1},{4,6},{6,4},{5,7},{7,5},{8,10},{10,8},{9,1... | collective-permute-start | bytes 1769480 | tf_op jit(solution)/shard_map/ppermute | solution.py:1031
  72.2 27.0 %collective-permute-start.8 = (bf16[2,2,2,2,24,1664]{5,4,3,2,1,0:T(8,128)(2,1)}, bf16[2,2,2,2,24,1664]{5,4,3,2,1,0:T(8,128)(2,1)}, u32[]{:S(2)}, u32[]{:S(2)}) collective-permute-start(bf16[2,2,2,2,24,1664]{5,4,3,2,1,0:T(8,128)(2,1)} %broadcast_select_fusion), channel_id=1, source_target_pairs={{0,1},{1,0},{2,3},{3,2},{4,5},{5,4},{6,7},{7,6},{8,9},{9,8},{10,11... | collective-permute-start | bytes 3833864 | tf_op jit(solution)/shard_map/ppermute | solution.py:1031
  83.0 12.9 %collective-permute-start.5 = (bf16[2,2,2,2,24,1536]{5,4,3,2,1,0:T(8,128)(2,1)}, bf16[2,2,2,2,24,1536]{5,4,3,2,1,0:T(8,128)(2,1)}, u32[]{:S(2)}, u32[]{:S(2)}) collective-permute-start(bf16[2,2,2,2,24,1536]{5,4,3,2,1,0:T(8,128)(2,1)} %broadcast_select_fusion.1), channel_id=1, source_target_pairs={{0,1},{1,0},{2,3},{3,2},{4,5},{5,4},{6,7},{7,6},{8,9},{9,8},{10,11... | collective-permute-start | bytes 3538952 | tf_op jit(solution)/shard_map/ppermute | solution.py:1031
  84.1 42.9 %collective-permute-start.10 = (bf16[384,1536]{1,0:T(8,128)(2,1)}, bf16[384,1536]{1,0:T(8,128)(2,1)S(1)}, u32[]{:S(2)}, u32[]{:S(2)}) collective-permute-start(bf16[384,1536]{1,0:T(8,128)(2,1)} %slice.70), channel_id=1, source_target_pairs={{0,2},{2,0},{1,3},{3,1},{4,6},{6,4},{5,7},{7,5},{8,10},{10,8},{9,1... | collective-permute-start | bytes 3538952 | tf_op jit(solution)/shard_map/ppermute | solution.py:1105
  86.5 40.5 %collective-permute-start.11 = (bf16[432,768]{1,0:T(8,128)(2,1)}, bf16[432,768]{1,0:T(8,128)(2,1)}, u32[]{:S(2)}, u32[]{:S(2)}) collective-permute-start(bf16[432,768]{1,0:T(8,128)(2,1)} %slice.71), channel_id=1, source_target_pairs={{0,2},{2,0},{1,3},{3,1},{4,6},{6,4},{5,7},{7,5},{8,10},{10,8},{9,1... | collective-permute-start | bytes 1990664 | tf_op jit(solution)/shard_map/ppermute | solution.py:1105
  127.0 7.1 %copy-start.17 = (bf16[384,1536]{1,0:T(8,128)(2,1)}, bf16[384,1536]{1,0:T(8,128)(2,1)S(1)}, u32[]{:S(2)}) copy-start(bf16[384,1536]{1,0:T(8,128)(2,1)S(1)} %collective-permute-done.10) | copy-start | bytes 3538948
  127.0 46.6 %all-to-all-start.1 = ((bf16[16,64,768]{2,1,0:T(8,128)(2,1)}), bf16[16,64,768]{2,1,0:T(8,128)(2,1)}, u32[]{:S(2)}, u32[]{:S(2)}) async-start(bf16[16,64,768]{2,1,0:T(8,128)(2,1)} %bitcast.92), calls=%async_computation.1 | async-start | bytes 3145728 | tf_op jit(solution)/shard_map/all_to_all | solution.py:1006
  134.2 39.5 %collective-permute-start.12 = (bf16[1104,768]{1,0:T(8,128)(2,1)}, bf16[1104,768]{1,0:T(8,128)(2,1)S(1)}, u32[]{:S(2)}, u32[]{:S(2)}) collective-permute-start(bf16[1104,768]{1,0:T(8,128)(2,1)} %slice.72), channel_id=1, source_target_pairs={{0,2},{2,0},{1,3},{3,1},{4,6},{6,4},{5,7},{7,5},{8,10},{10,8},{9,1... | collective-permute-start | bytes 5087240 | tf_op jit(solution)/shard_map/ppermute | solution.py:1105
  173.7 40.1 %all-to-all-start.2 = ((bf16[16,64,768]{2,1,0:T(8,128)(2,1)}), bf16[16,64,768]{2,1,0:T(8,128)(2,1)S(1)}, u32[]{:S(2)}, u32[]{:S(2)}) async-start(bf16[16,64,768]{2,1,0:T(8,128)(2,1)} %bitcast.91), calls=%async_computation.2 | async-start | bytes 3145728 | tf_op jit(solution)/shard_map/all_to_all | solution.py:1006
  213.8 7.1 %copy-start.13 = (bf16[16,64,768]{2,1,0:T(8,128)(2,1)}, bf16[16,64,768]{2,1,0:T(8,128)(2,1)S(1)}, u32[]{:S(2)}) copy-start(bf16[16,64,768]{2,1,0:T(8,128)(2,1)S(1)} %all-to-all-done.2) | copy-start | bytes 4718596
  213.8 41.5 %all-to-all-start.4 = ((bf16[16,64,768]{2,1,0:T(8,128)(2,1)}), bf16[16,64,768]{2,1,0:T(8,128)(2,1)S(1)}, u32[]{:S(2)}, u32[]{:S(2)}) async-start(bf16[16,64,768]{2,1,0:T(8,128)(2,1)} %get-tuple-element.98), calls=%async_computation.4 | async-start | bytes 3145728 | tf_op jit(solution)/shard_map/all_to_all | solution.py:1006
  255.3 24.5 %copy-start.24 = (bf16[16,64,768]{2,1,0:T(8,128)(2,1)}, bf16[16,64,768]{2,1,0:T(8,128)(2,1)S(1)}, u32[]{:S(2)}) copy-start(bf16[16,64,768]{2,1,0:T(8,128)(2,1)S(1)} %all-to-all-done.4) | copy-start | bytes 4718596
  255.3 44.9 %all-to-all-start.5 = ((bf16[16,64,768]{2,1,0:T(8,128)(2,1)}), bf16[16,64,768]{2,1,0:T(8,128)(2,1)S(1)}, u32[]{:S(2)}, u32[]{:S(2)}) async-start(bf16[16,64,768]{2,1,0:T(8,128)(2,1)} %get-tuple-element.89._early), calls=%async_computation.5 | async-start | bytes 3145728 | tf_op jit(solution)/shard_map/all_to_all | solution.py:1006
  279.9 20.3 %collective-permute-start.13 = (bf16[256,1536]{1,0:T(8,128)(2,1)}, bf16[256,1536]{1,0:T(8,128)(2,1)}, u32[]{:S(2)}, u32[]{:S(2)}) collective-permute-start(bf16[256,1536]{1,0:T(8,128)(2,1)} %bitcast.101), channel_id=1, source_target_pairs={{0,2},{2,0},{1,3},{3,1},{4,6},{6,4},{5,7},{7,5},{8,10},{10,8},{9,1... | collective-permute-start | bytes 2359304 | tf_op jit(solution)/shard_map/ppermute | solution.py:1108
  301.4 66.2 %all-to-all-start.3 = ((bf16[16,128,768]{2,1,0:T(8,128)(2,1)}), bf16[16,128,768]{2,1,0:T(8,128)(2,1)S(1)}, u32[]{:S(2)}, u32[]{:S(2)}) async-start(bf16[16,128,768]{2,1,0:T(8,128)(2,1)} %get-tuple-element.93), calls=%async_computation.3 | async-start | bytes 6291456 | tf_op jit(solution)/shard_map/all_to_all | solution.py:1006
  307.1 53.8 %collective-permute-start.14 = (bf16[512,1536]{1,0:T(8,128)(2,1)}, bf16[512,1536]{1,0:T(8,128)(2,1)S(1)}, u32[]{:S(2)}, u32[]{:S(2)}) collective-permute-start(bf16[512,1536]{1,0:T(8,128)(2,1)} %bitcast.99), channel_id=1, source_target_pairs={{0,2},{2,0},{1,3},{3,1},{4,6},{6,4},{5,7},{7,5},{8,10},{10,8},{9,1... | collective-permute-start | bytes 4718600 | tf_op jit(solution)/shard_map/ppermute | solution.py:1108
  308.7 52.2 %collective-permute-start.15 = (bf16[1536,256]{1,0:T(8,128)(2,1)}, bf16[1536,256]{1,0:T(8,128)(2,1)S(1)}, u32[]{:S(2)}, u32[]{:S(2)}) collective-permute-start(bf16[1536,256]{1,0:T(8,128)(2,1)} %bitcast.100), channel_id=1, source_target_pairs={{0,2},{2,0},{1,3},{3,1},{4,6},{6,4},{5,7},{7,5},{8,10},{10,8},{9,1... | collective-permute-start | bytes 2359304 | tf_op jit(solution)/shard_map/ppermute | solution.py:1108
  360.9 4.0 collective-permute-start.16
  361.0 20.9 %collective-permute-start.18 = (bf16[2,8,24,1664]{3,2,1,0:T(8,128)(2,1)}, bf16[2,8,24,1664]{3,2,1,0:T(8,128)(2,1)}, u32[]{:S(2)}, u32[]{:S(2)}) collective-permute-start(bf16[2,8,24,1664]{3,2,1,0:T(8,128)(2,1)} %get-tuple-element.115), channel_id=1, source_target_pairs={{0,1},{1,0},{2,3},{3,2},{4,5},{5,4},{6,7},{7,6},{8,9},{9,8},{10,11... | collective-permute-start | bytes 3833864 | tf_op jit(solution)/shard_map/ppermute | solution.py:1232
  361.5 36.7 %collective-permute-start.19 = (bf16[1536,512]{1,0:T(8,128)(2,1)}, bf16[1536,512]{1,0:T(8,128)(2,1)}, u32[]{:S(2)}, u32[]{:S(2)}) collective-permute-start(bf16[1536,512]{1,0:T(8,128)(2,1)} %bitcast.98), channel_id=1, source_target_pairs={{0,2},{2,0},{1,3},{3,1},{4,6},{6,4},{5,7},{7,5},{8,10},{10,8},{9,1... | collective-permute-start | bytes 4718600 | tf_op jit(solution)/shard_map/ppermute | solution.py:1108
  367.6 48.4 %all-to-all-start.6 = ((bf16[8,2,24,1536]{3,2,1,0:T(8,128)(2,1)}), bf16[8,2,24,1536]{3,2,1,0:T(8,128)(2,1)}, u32[]{:S(2)}, u32[]{:S(2)}) async-start(bf16[8,2,24,1536]{3,2,1,0:T(8,128)(2,1)} %convert_add_fusion.2), calls=%async_computation.6 | async-start | bytes 2359296 | tf_op jit(solution)/shard_map/all_to_all | solution.py:1242
  384.0 14.2 %copy-start.14 = (bf16[2,8,24,1664]{3,2,1,0:T(8,128)(2,1)}, bf16[2,8,24,1664]{3,2,1,0:T(8,128)(2,1)S(1)}, u32[]{:S(2)}) copy-start(bf16[2,8,24,1664]{3,2,1,0:T(8,128)(2,1)S(1)} %add_convert_fusion) | copy-start | bytes 3833860
  398.2 15.7 %collective-permute-start.20 = (bf16[8,24,1664]{2,1,0:T(8,128)(2,1)S(1)}, bf16[8,24,1664]{2,1,0:T(8,128)(2,1)}, u32[]{:S(2)}, u32[]{:S(2)}) collective-permute-start(bf16[8,24,1664]{2,1,0:T(8,128)(2,1)S(1)} %dynamic-slice_bitcast_fusion), channel_id=1, source_target_pairs={{0,2},{2,0},{1,3},{3,1},{4,6},{6,4},{5,7},{7,5},{8,10},{10,8},{9,1... | collective-permute-start | bytes 1916936 | tf_op jit(solution)/shard_map/ppermute | solution.py:1048
  406.6 7.3 %copy-start.15 = (bf16[2,8,24,1664]{3,2,1,0:T(8,128)(2,1)S(1)}, bf16[2,8,24,1664]{3,2,1,0:T(8,128)(2,1)}, u32[]{:S(2)}) copy-start(bf16[2,8,24,1664]{3,2,1,0:T(8,128)(2,1)} %copy-done.14) | copy-start | bytes 3833860
  417.4 21.3 %all-to-all-start.7 = ((bf16[8,24,1664]{2,1,0:T(8,128)(2,1)}), bf16[8,24,1664]{2,1,0:T(8,128)(2,1)S(1)}, u32[]{:S(2)}, u32[]{:S(2)}) async-start(bf16[8,24,1664]{2,1,0:T(8,128)(2,1)} %convert_add_fusion.3), calls=%async_computation.7 | async-start | bytes 1277952 | tf_op jit(solution)/shard_map/all_to_all | solution.py:1242
  427.7 31.0 %copy-start.26 = (f32[24,16]{0,1:T(8,128)S(1)}, f32[24,16]{0,1:T(8,128)}, u32[]{:S(2)}) copy-start(f32[24,16]{0,1:T(8,128)} %param.29) | copy-start | bytes 4612
  427.7 31.0 %copy-start.27 = (f32[24,16]{0,1:T(8,128)S(1)}, f32[24,16]{0,1:T(8,128)}, u32[]{:S(2)}) copy-start(f32[24,16]{0,1:T(8,128)} %param.39) | copy-start | bytes 4612
  427.7 31.0 %copy-start.28 = (f32[24,16]{0,1:T(8,128)S(1)}, f32[24,16]{0,1:T(8,128)}, u32[]{:S(2)}) copy-start(f32[24,16]{0,1:T(8,128)} %param.38) | copy-start | bytes 4612
  427.7 4.5 collective-permute-start.17
  432.3 29.2 %copy-start.29 = (f32[24,4]{0,1:T(4,128)S(1)}, f32[24,4]{0,1:T(4,128)}, u32[]{:S(2)}) copy-start(f32[24,4]{0,1:T(4,128)} %param.26) | copy-start | bytes 1156
  432.3 29.2 %copy-start.32 = (f32[24,4]{0,1:T(4,128)S(1)}, f32[24,4]{0,1:T(4,128)}, u32[]{:S(2)}) copy-start(f32[24,4]{0,1:T(4,128)} %param.33) | copy-start | bytes 1156
  438.8 35.3 %slice-start.1 = ((s8[4718592]{0:T(1024)(128)(4,1)}), s8[524288]{0:T(1024)(128)(4,1)S(1)}, s32[]{:S(2)}) async-start(s8[4718592]{0:T(1024)(128)(4,1)} %bitcast.74), calls=%async_computation.10 | async-start | bytes 1048576
  443.7 10.8 %all-to-all-start.8 = ((f32[32,1,128]{2,1,0:T(1,128)}), f32[32,1,128]{2,1,0:T(1,128)S(1)}, u32[]{:S(2)}, u32[]{:S(2)}) async-start(f32[32,1,128]{2,1,0:T(1,128)} %broadcast_in_dim.259), calls=%async_computation.8 | async-start | bytes 32768 | tf_op jit(solution)/shard_map/all_to_all | solution.py:1262
  462.7 11.4 %slice-start.2 = ((s8[4718592]{0:T(1024)(128)(4,1)}), s8[4194304]{0:T(1024)(128)(4,1)S(1)}, s32[]{:S(2)}) async-start(s8[4718592]{0:T(1024)(128)(4,1)} %bitcast.74), calls=%async_computation.11 | async-start | bytes 8388608
  462.7 12.2 %copy-start.12 = (bf16[512,1536]{1,0:T(8,128)(2,1)S(1)}, bf16[512,1536]{1,0:T(8,128)(2,1)}, u32[]{:S(2)}) copy-start(bf16[512,1536]{1,0:T(8,128)(2,1)} %copy-done.10) | copy-start | bytes 4718596
  (18 other events, 61.2 us)
